TPU v7x, 256 devices: a whole 4x4x8 slice. The times are simulated.
256 devices in a mesh: rep: 8 (over y, core), exp: 32 (over x, z).
Axes of the slice: x: 4, y: 4, z: 8, core: 2. Of those that a mesh axis runs over, the one named last changes fastest.
Arguments:
- grad_out: bfloat16 [8, 4096, 2048], P('rep', 'exp'), may hold values from -2 to 2
- gates: float32 [8, 4096, 8], P('rep', 'exp'), may hold values from 0.05 to 0.5
- routes: int32 [8, 4096, 8], P('rep', 'exp'), may hold values from 0 to 31, all different within a row; in each aligned block of 128 rows (0 to 127, 128 to 255, ..., all dimensions but the last counted through in order) at most 64 rows name the same one
- hidden: bfloat16 [8, 32, 2048, 768], P('rep', 'exp'), may hold values from -6 to 6
- error: bfloat16 [8, 32, 768, 2048], P('rep', 'exp'), may hold values from -6 to 6
- q_init: float32 [32, 32, 2048], P('exp'), may hold values from -6 to 6
Outputs:
- new_error: bfloat16 [8, 32, 768, 2048], P('rep', 'exp')
- p_factor: float32 [32, 32, 768], P('exp')
- q_factor: float32 [32, 32, 2048], P('exp')
Inputs may be any that keep to these rules, and one draw needn't show every extreme that they name: `routes`: each row names 8 different experts; among the tokens of one device at most 64 name one expert, and in every draw exactly 64 do for some expert.
All inputs are finite; a program needn't handle non-finite values.
Results may differ from a plain program's by a relative error of at most 0.015.
Values may be sent and summed in bfloat16 or wider, within the bound.
No kernel may reach another device: no remote copies, remote signals or barrier semaphores. Data moves between devices by JAX's collectives and lax.ppermute only.
A program may use at most 128 MiB of HBM per device.

v0:
```python
import jax
import jax.numpy as jnp
from jax import lax
from jax.sharding import PartitionSpec as P


def orthonormal(rows):
    count = rows.shape[0]
    index = jnp.arange(count, dtype=jnp.int32)

    def step(i, current):
        vector = current[i]
        vector = vector / jnp.sqrt(jnp.sum(vector * vector))
        coeffs = jnp.dot(current, vector, precision=lax.Precision.HIGHEST)
        current = current - jnp.where(index > i, coeffs, 0.0)[:, None] * vector[None, :]
        return current.at[i].set(vector)

    return lax.fori_loop(0, count, step, rows)


def body(grad_out, gates, routes, hidden, error, q_init):
    groups = lax.axis_size("exp")
    local_experts = hidden.shape[1]
    slots = hidden.shape[2]
    cap = slots // groups
    experts = local_experts * groups
    width = grad_out.shape[2]
    held = hidden[0]
    ids = routes[0].reshape(-1)
    onehot = (ids[:, None] == jnp.arange(experts, dtype=jnp.int32)[None, :]).astype(jnp.int32)
    position = jnp.sum((jnp.cumsum(onehot, axis=0) - onehot) * onehot, axis=1)
    slot = ids * cap + position
    scaled = (gates[0][:, :, None] * grad_out[0][:, None, :].astype(jnp.float32)).astype(
        jnp.bfloat16
    )
    outgoing = (
        jnp.zeros((experts * cap, width), jnp.bfloat16).at[slot].set(scaled.reshape(-1, width))
    )
    outgoing = outgoing.reshape(experts, cap, width)
    grad_w = jnp.einsum(
        "esf,esd->efd",
        held,
        lax.all_to_all(outgoing, "exp", split_axis=0, concat_axis=1, tiled=True),
        preferred_element_type=jnp.float32,
    )
    acc = grad_w + error[0].astype(jnp.float32)
    p_local = jnp.einsum("ekd,efd->ekf", q_init, acc, precision=lax.Precision.HIGHEST)
    p_total = lax.psum(p_local, "rep")
    p_hat = jax.vmap(orthonormal)(p_total)
    q_local = jnp.einsum("ekf,efd->ekd", p_hat, acc, precision=lax.Precision.HIGHEST)
    q_mean = lax.psum(q_local.astype(jnp.bfloat16), "rep").astype(jnp.float32) / lax.axis_size(
        "rep"
    )
    approx = jnp.einsum("ekf,ekd->efd", p_hat, q_mean, precision=lax.Precision.HIGHEST)
    new_error = (acc - approx).astype(jnp.bfloat16)[None]
    return (new_error, p_hat, q_mean)


def solution(mesh):
    return jax.shard_map(
        body,
        mesh=mesh,
        in_specs=(
            P("rep", "exp", None),
            P("rep", "exp", None),
            P("rep", "exp", None),
            P("rep", "exp", None, None),
            P("rep", "exp", None, None),
            P("exp", None, None),
        ),
        out_specs=(P("rep", "exp", None, None), P("exp", None, None), P("exp", None, None)),
        check_vma=False,
    )
```

profile of v0, /device:TPU:1, one launch (start us, length us, event | category | flops | bytes accessed | tf_op | source)
XLA Modules:
  0.0 704.2 jit_solution(5289988256843290305)
XLA Ops:
  9.0 9.0 %reduce-window.6 = s32[32,8,128]{2,1,0:T(8,128)S(1)} reduce-window(s32[32,8,128]{2,1,0:T(8,128)S(1)} %fusion.19, s32[]{:T(128)} %constant.87.clone.1), window={size=1x1x128 pad=0_0x0_0x127_0}, to_apply=%region_0.0 | reduce-window | flops 4161536 | bytes 262148 | tf_op jit(solution)/shard_map/reduce-window
  18.7 2.1 bitcast_convert_fusion
  21.7 12.1 %scatter_custom_fusion = bf16[2048,2048]{1,0:T(8,128)(2,1)} fusion(s32[1024]{0:T(1024)S(1)} %bitcast.95, f32[128,2048]{1,0:T(8,128)} %bitcast_convert_fusion, f32[1024]{0:T(1024)S(1)} %mul.94, bf16[]{:T(256)} %constant.85.clone.1), kind=kCustom, calls=%fused_computation.16 | custom fusion | flops 4194304 | bytes 9441282 | tf_op jit(solution)/shard_map/scatter | solution.py:37
  33.8 12.0 %all-to-all-start = ((bf16[32,64,2048]{2,1,0:T(8,128)(2,1)}), bf16[32,64,2048]{2,1,0:T(8,128)(2,1)}, u32[]{:S(2)}, u32[]{:S(2)}) async-start(bf16[32,64,2048]{2,1,0:T(8,128)(2,1)} %bitcast.89), calls=%async_computation | async-start | bytes 16777216 | tf_op jit(solution)/shard_map/all_to_all | solution.py:43
  46.0 4.6 copy.18
  50.7 183.3 %all-to-all-done = bf16[32,64,2048]{2,1,0:T(8,128)(2,1)} async-done(((bf16[32,64,2048]{2,1,0:T(8,128)(2,1)}), bf16[32,64,2048]{2,1,0:T(8,128)(2,1)}, u32[]{:S(2)}, u32[]{:S(2)}) %all-to-all-start) | async-done | bytes 8388640 | tf_op jit(solution)/shard_map/all_to_all | solution.py:43
  234.0 10.1 %convert_add_fusion = f32[768,2048]{0,1:T(8,128)S(1)} fusion(bf16[2048,2048]{1,0:T(8,128)(2,1)} %bitcast.7, bf16[1,1,768,2048]{2,3,1,0:T(8,128)(2,1)} %copy.18, bf16[1,1,2048,768]{3,2,1,0:T(8,128)(2,1)S(1)} %copy-done), kind=kOutput, calls=%fused_computation.14 | convolution fusion | flops 6445596672 | bytes 20971520 | tf_op jit(solution)/shard_map/esf,esd->efd/dot_general | solution.py:40
  244.1 2.7 copy-done.1
  246.8 4.5 convolution_bitcast_fusion.1
  251.6 67.0 %all-reduce.3.cloned.1.call-done = f32[1,32,768]{2,1,0:T(8,128)} async-done(((f32[1,32,768]{2,1,0:T(8,128)}), f32[1,32,768]{2,1,0:T(8,128)}) %all-reduce.3.cloned.1.call-update) | async-done | bytes 98320 | tf_op jit(solution)/shard_map/psum | solution.py:48
  318.6 291.4 %while.16 = (s32[]{:T(128)}, f32[1,32,768]{2,1,0:T(8,128)}, s32[]{:T(128)}, s32[1]{0:T(128)}, s32[3]{0:T(128)S(1)}, /*index=5*/s32[]{:T(128)}) while((s32[]{:T(128)}, f32[1,32,768]{2,1,0:T(8,128)}, s32[]{:T(128)}, s32[1]{0:T(128)}, s32[3]{0:T(128)S(1)}, /*index=5*/s32[]{:T(128)}) %tuple.61), condition=%wide.region_8.9_spmd.clone, body=%wide.region_5.8_spmd.clone.sunk | while | flops 347220 | bytes 329103 | solution.py:18
  322.6 1.6 multiply_subtract_fusion.2
  331.7 1.6 multiply_subtract_fusion.2
  340.8 1.6 multiply_subtract_fusion.2
  349.9 1.6 multiply_subtract_fusion.2
  359.0 1.6 multiply_subtract_fusion.2
  361.4 1.4 broadcast_select_fusion.2
  368.1 1.6 multiply_subtract_fusion.2
  377.2 1.6 multiply_subtract_fusion.2
  386.3 1.6 multiply_subtract_fusion.2
  395.5 1.6 multiply_subtract_fusion.2
  404.6 1.6 multiply_subtract_fusion.2
  413.7 1.6 multiply_subtract_fusion.2
  422.8 1.6 multiply_subtract_fusion.2
  431.9 1.6 multiply_subtract_fusion.2
  441.0 1.6 multiply_subtract_fusion.2
  450.1 1.6 multiply_subtract_fusion.2
  459.2 1.6 multiply_subtract_fusion.2
  468.4 1.6 multiply_subtract_fusion.2
  477.5 1.6 multiply_subtract_fusion.2
  486.6 1.6 multiply_subtract_fusion.2
  495.7 1.6 multiply_subtract_fusion.2
  504.8 1.6 multiply_subtract_fusion.2
  513.9 1.6 multiply_subtract_fusion.2
  523.0 1.6 multiply_subtract_fusion.2
  532.1 1.6 multiply_subtract_fusion.2
  541.2 1.6 multiply_subtract_fusion.2
  550.3 1.6 multiply_subtract_fusion.2
  559.4 1.6 multiply_subtract_fusion.2
  568.5 1.6 multiply_subtract_fusion.2
  577.6 1.6 multiply_subtract_fusion.2
  586.7 1.6 multiply_subtract_fusion.2
  595.9 1.6 multiply_subtract_fusion.2
  605.0 1.6 multiply_subtract_fusion.2
  610.1 9.2 %fusion.13 = bf16[1,32,2048]{2,1,0:T(8,128)(2,1)} fusion(f32[768,2048]{0,1:T(8,128)} %copy-done.1, f32[1,32,768]{2,1,0:T(8,128)} %get-tuple-element.155), kind=kOutput, calls=%fused_computation.23 | convolution fusion | flops 604045312 | bytes 6520832 | tf_op jit(solution)/shard_map/ekf,efd->ekd/dot_general | solution.py:50
  619.3 63.2 %all-reduce.5.cloned.1.call-done = bf16[1,32,2048]{2,1,0:T(8,128)(2,1)} async-done(((bf16[1,32,2048]{2,1,0:T(8,128)(2,1)}), bf16[1,32,2048]{2,1,0:T(8,128)(2,1)}) %all-reduce.5.cloned.1.call-update) | async-done | bytes 131088 | tf_op jit(solution)/shard_map/psum | solution.py:51
  683.4 8.6 %fusion.12 = bf16[1,1,768,2048]{2,3,1,0:T(8,128)(2,1)} fusion(f32[768,2048]{0,1:T(8,128)} %copy-done.1, f32[1,32,2048]{2,1,0:T(8,128)S(1)} %convert_multiply_fusion, f32[1,32,768]{2,1,0:T(8,128)S(1)} %copy-done.2), kind=kOutput, calls=%fused_computation.21 | convolution fusion | flops 607125504 | bytes 9797632 | tf_op jit(solution)/shard_map/ekf,ekd->efd/dot_general | solution.py:54
  692.1 4.6 copy.20
  (257 shorter events, 220.5 us)
Async XLA Ops:
  7.2 226.9 %copy-start = (bf16[1,1,2048,768]{3,2,1,0:T(8,128)(2,1)S(1)}, bf16[1,1,2048,768]{3,2,1,0:T(8,128)(2,1)}, u32[]{:S(2)}) copy-start(bf16[1,1,2048,768]{3,2,1,0:T(8,128)(2,1)} %param.13) | copy-start | bytes 9437188
  33.8 200.2 %all-to-all-start = ((bf16[32,64,2048]{2,1,0:T(8,128)(2,1)}), bf16[32,64,2048]{2,1,0:T(8,128)(2,1)}, u32[]{:S(2)}, u32[]{:S(2)}) async-start(bf16[32,64,2048]{2,1,0:T(8,128)(2,1)} %bitcast.89), calls=%async_computation | async-start | bytes 16777216 | tf_op jit(solution)/shard_map/all_to_all | solution.py:43
  45.8 272.8 %all-reduce.3.cloned.1.call-start = ((), (), s32[]{:S(2)}) async-start(), calls=%async_computation.1 | async-start | bytes 196608 | tf_op jit(solution)/shard_map/psum | solution.py:48
  234.0 12.7 %copy-start.4 = (f32[1,32,2048]{2,1,0:T(8,128)S(1)}, f32[1,32,2048]{2,1,0:T(8,128)}, u32[]{:S(2)}) copy-start(f32[1,32,2048]{2,1,0:T(8,128)} %param.15) | copy-start | bytes 786436
  244.1 2.7 copy-start.1
  246.8 71.8 %copy-start.5 = (s32[3]{0:T(128)S(1)}, s32[3]{0:T(128)}, u32[]{:S(2)}) copy-start(s32[3]{0:T(128)} %constant.82.clone.2) | copy-start | bytes 40
  251.3 431.2 %all-reduce.5.cloned.1.call-start = ((), (), s32[]{:S(2)}) async-start(), calls=%async_computation.2 | async-start | bytes 262144 | tf_op jit(solution)/shard_map/psum | solution.py:51
  610.1 73.4 %copy-start.2 = (f32[1,32,768]{2,1,0:T(8,128)S(1)}, f32[1,32,768]{2,1,0:T(8,128)}, u32[]{:S(2)}) copy-start(f32[1,32,768]{2,1,0:T(8,128)} %get-tuple-element.155) | copy-start | bytes 294916
  683.4 13.3 %copy-start.3 = (f32[1,32,2048]{2,1,0:T(8,128)}, f32[1,32,2048]{2,1,0:T(8,128)S(1)}, u32[]{:S(2)}) copy-start(f32[1,32,2048]{2,1,0:T(8,128)S(1)} %convert_multiply_fusion) | copy-start | bytes 786436
Sparse Core Ops, SparseCore 0:
  251.4 67.1 all-reduce.2
  619.4 63.0 all-reduce.4
where the time goes:
time: 716 us; the launch traced here: 704 us
  waiting for transfers between devices  314 us (44%)
  other arithmetic  217 us (30%)
  matrix products  66 us (9%)
  local copies, waits for them, and re-layouts  58.5 us (8%)
  loops' own time  22.4 us (3%)
  between operations  14.1 us (2%)
  starting transfers between devices  12.5 us (2%)
    all_to_all x1, waiting for transfers between devices, body(): lax.all_to_all(outgoing, 'exp', split_axis=0, concat_axis=1, tiled=True)  183 us
    another operation x67, other arithmetic  76.4 us
    psum x1, waiting for transfers between devices, body(): p_total = lax.psum(p_local, 'rep')  67 us
    psum x1, waiting for transfers between devices, body(): lax.psum(q_local.astype(jnp.bfloat16), 'rep').astype(jnp.float32)  63.2 us
    sub x32, other arithmetic, step(): current - jnp.where(index > i, coeffs, 0.0)[:, None] * vector[None, :]  52.6 us
    reduce_sum x32, other arithmetic, step(): vector = vector / jnp.sqrt(jnp.sum(vector * vector))  44.5 us
    scatter x32, local copies, waits for them, and re-layouts, step(): return current.at[i].set(vector)  43.4 us
    dot_general x32, matrix products, step(): coeffs = jnp.dot(current, vector, precision=lax.Precision.HIGHEST)  33.6 us
  transfers between devices with their start and end apart: 3, of which 3 were waited for; matrix products, arithmetic and copies ran while one was open for 1% of the time, Pallas kernels for 0%

commit v1 on v0

v1 whole, which is shorter than its diff:
```python
import functools

import jax
import jax.numpy as jnp
from jax import lax
from jax.experimental import pallas as pl
from jax.experimental.pallas import tpu as pltpu
from jax.sharding import PartitionSpec as P

F32 = jnp.float32
BF16 = jnp.bfloat16

NX, NZ = 4, 8
TOK = 128
CAP = 64
META = 8
ROWS = TOK + META
GROUPS = ((0,), (1, 7), (2, 6), (3, 5), (4,))


def move(block, dx, dz):
    pairs = []
    for x in range(NX):
        for z in range(NZ):
            pairs.append((x * NZ + z, ((x + dx) % NX) * NZ + (z + dz) % NZ))
    return lax.ppermute(block, "exp", pairs)


def select_kernel(counts, experts, ids_ref, *refs):
    blocks, out_ref = refs[: len(counts)], refs[-1]
    total = sum(counts) * CAP
    row = lax.broadcasted_iota(jnp.int32, (TOK, TOK), 0)
    col = lax.broadcasted_iota(jnp.int32, (TOK, TOK), 1)
    before = jnp.where(row < col, 1.0, 0.0).astype(BF16)
    slot = lax.broadcasted_iota(jnp.int32, (CAP, TOK), 0).astype(F32)
    place = 0
    for ref, count in zip(blocks, counts):
        for b in range(count):
            base = b * ROWS
            meta = ref[base + TOK : base + ROWS, 0 : 4 * TOK].astype(F32)
            routes = meta[:, 0:TOK]
            gates = (meta[:, TOK : 2 * TOK] + meta[:, 2 * TOK : 3 * TOK]) + meta[:, 3 * TOK :]
            gate, live = [], []
            for e in range(experts):
                match = routes == ids_ref[e].astype(F32)
                gate.append(jnp.sum(jnp.where(match, gates, 0.0), axis=0, keepdims=True))
                live.append(jnp.sum(jnp.where(match, 1.0, 0.0), axis=0, keepdims=True))
            alive = jnp.concatenate(live + [jnp.zeros((8 - experts, TOK), F32)], axis=0)
            position = jnp.dot(alive.astype(BF16), before, preferred_element_type=F32)
            picks, scales = [], []
            for e in range(experts):
                pick = jnp.where((slot == position[e : e + 1]) & (live[e] > 0.0), 1.0, 0.0)
                picks.append(pick)
                scales.append(jnp.sum(pick * gate[e], axis=1, keepdims=True))
            pick = jnp.concatenate(picks, axis=0).astype(BF16)
            scale = jnp.concatenate(scales, axis=0)
            for c in range(0, ref.shape[1], 512):
                rows = jnp.dot(
                    pick, ref[base : base + TOK, c : c + 512], preferred_element_type=F32
                )
                rows = (rows * scale).astype(BF16)
                for e in range(experts):
                    first = e * total + place
                    out_ref[first : first + CAP, c : c + 512] = rows[e * CAP : (e + 1) * CAP]
            place += CAP


def select(blocks, ids, after=()):
    counts = tuple(b.shape[0] // ROWS for b in blocks)
    width = blocks[0].shape[1]
    experts = ids.shape[0]
    total = sum(counts)
    return pl.pallas_call(
        functools.partial(select_kernel, counts, experts),
        in_specs=[pl.BlockSpec(memory_space=pltpu.SMEM)]
        + [pl.BlockSpec(memory_space=pltpu.VMEM)] * len(blocks)
        + [pl.BlockSpec(memory_space=pl.ANY)] * len(after),
        out_specs=pl.BlockSpec(memory_space=pltpu.VMEM),
        out_shape=jax.ShapeDtypeStruct((experts * total * CAP, width), BF16),
        cost_estimate=pl.CostEstimate(
            flops=2 * total * experts * CAP * TOK * width,
            bytes_accessed=total * (ROWS + CAP * experts) * width * 2,
            transcendentals=0,
        ),
        compiler_params=pltpu.CompilerParams(vmem_limit_bytes=32 << 20),
        name="select",
    )(ids, *blocks, *after)


def pack_kernel(experts, ids_ref, grad_ref, routes_ref, gates_ref, block_ref, out_ref):
    gates = gates_ref[...]
    high = gates.astype(BF16)
    rest = gates - high.astype(F32)
    mid = rest.astype(BF16)
    low = (rest - mid.astype(F32)).astype(BF16)
    meta = jnp.concatenate([routes_ref[...].astype(F32).astype(BF16), high, mid, low], axis=1)
    block_ref[0:TOK, :] = grad_ref[...]
    block_ref[TOK:ROWS, 0 : 4 * TOK] = meta
    block_ref[TOK:ROWS, 4 * TOK :] = jnp.zeros((META, grad_ref.shape[1] - 4 * TOK), BF16)
    select_kernel((1,), experts, ids_ref, block_ref, out_ref)


def pack(grad, routes, gates, ids):
    vmem = pl.BlockSpec(memory_space=pltpu.VMEM)
    width = grad.shape[1]
    experts = ids.shape[0]
    return pl.pallas_call(
        functools.partial(pack_kernel, experts),
        in_specs=[pl.BlockSpec(memory_space=pltpu.SMEM)] + [vmem] * 3,
        out_specs=[vmem] * 2,
        out_shape=[
            jax.ShapeDtypeStruct((ROWS, width), BF16),
            jax.ShapeDtypeStruct((experts * CAP, width), BF16),
        ],
        cost_estimate=pl.CostEstimate(flops=0, bytes_accessed=2 << 20, transcendentals=0),
        compiler_params=pltpu.CompilerParams(vmem_limit_bytes=32 << 20),
        name="pack",
    )(ids, grad, routes, gates)


def split(value):
    high = value.astype(BF16)
    return high, (value - high.astype(F32)).astype(BF16)


def turn(order, hidden_ref, turned, sources):
    for j in range(sources // 2):
        pair = [
            hidden_ref[pl.ds(pl.multiple_of(order[2 * j + k] * CAP, CAP), CAP), :] for k in range(2)
        ]
        turned[:, j * 2 * CAP : (j + 1) * 2 * CAP] = jnp.concatenate(pair, axis=0).T


def left(acc, q_ref, total_ref):
    rank = q_ref.shape[1] // 2
    high, low = split(acc)
    both = jnp.dot(high, q_ref[...], preferred_element_type=F32)
    rest = jnp.dot(low, q_ref[:, :rank], preferred_element_type=F32)
    total_ref[...] += both[:, :rank] + (both[:, rank:] + rest)
    return high, low


def product_kernel(count, sources, order, hidden_ref, *refs):
    parts = refs[:count]
    init_ref, q_ref, acc_ref, p_ref, turned = refs[count:]

    @pl.when(pl.program_id(0) == 0)
    def _():
        p_ref[...] = jnp.zeros_like(p_ref)
        turn(order, hidden_ref, turned, sources)

    data = jnp.concatenate([p[...] for p in parts], axis=0)
    acc = init_ref[...].astype(F32) + jnp.dot(turned[...], data, preferred_element_type=F32)
    acc_ref[...] = acc
    left(acc, q_ref, p_ref)


def first_kernel(count, sources, order, hidden_ref, *refs):
    parts = refs[:count]
    init_ref, acc_ref, turned = refs[count:]

    @pl.when(pl.program_id(0) == 0)
    def _():
        turn(order, hidden_ref, turned, sources)

    data = jnp.concatenate([p[...] for p in parts], axis=0)
    acc_ref[...] = init_ref[...].astype(F32) + jnp.dot(
        turned[...], data, preferred_element_type=F32
    )


def product(order, hidden, parts, init, q_turned=None, first=0, tile=256):
    rows = init.shape[0]
    slots, feats = hidden.shape
    sources = order.shape[0]
    width = parts[0].shape[1]
    base = first // tile
    in_specs = [pl.BlockSpec((slots, feats), lambda i, order: (0, 0))]
    in_specs += [pl.BlockSpec((p.shape[0], tile), lambda i, order: (0, i)) for p in parts]
    in_specs += [pl.BlockSpec((rows, tile), lambda i, order: (0, i + base))]
    out_specs = [pl.BlockSpec((rows, tile), lambda i, order: (0, i))]
    out_shape = [jax.ShapeDtypeStruct((rows, width), F32)]
    args = (order, hidden, *parts, init)
    kernel = first_kernel
    if q_turned is not None:
        kernel = product_kernel
        thin = q_turned.shape[1]
        in_specs += [pl.BlockSpec((tile, thin), lambda i, order: (i + base, 0))]
        out_specs += [pl.BlockSpec((rows, thin // 2), lambda i, order: (0, 0))]
        out_shape += [jax.ShapeDtypeStruct((rows, thin // 2), F32)]
        args += (q_turned,)
    return pl.pallas_call(
        functools.partial(kernel, len(parts), sources),
        grid_spec=pltpu.PrefetchScalarGridSpec(
            num_scalar_prefetch=1,
            grid=(width // tile,),
            in_specs=in_specs,
            out_specs=out_specs,
            scratch_shapes=[pltpu.VMEM((feats, sources * CAP), BF16)],
        ),
        out_shape=out_shape,
        cost_estimate=pl.CostEstimate(
            flops=2 * feats * sources * CAP * width,
            bytes_accessed=rows * width * 8 + sources * CAP * (feats + width) * 2,
            transcendentals=0,
        ),
        compiler_params=pltpu.CompilerParams(vmem_limit_bytes=40 << 20),
        name="product",
    )(*args)


def left_kernel(count, sources, order, hidden_hbm, *refs):
    parts = refs[:count]
    q_ref, p_ref, out_ref, held, sem = refs[count:]
    copies = [
        pltpu.make_async_copy(
            hidden_hbm.at[pl.ds(pl.multiple_of(order[j] * CAP, CAP), CAP)],
            held.at[pl.ds(j * CAP, CAP)],
            sem.at[j],
        )
        for j in range(sources)
    ]
    for copy in copies:
        copy.start()
    data = jnp.concatenate([p[...] for p in parts], axis=0)
    rank = out_ref.shape[0]
    both = jnp.dot(data, q_ref[...], preferred_element_type=F32)
    high, low = split(both[:, :rank] + both[:, rank:])
    for copy in copies:
        copy.wait()
    more = lax.dot_general(
        jnp.concatenate([high, low], axis=1),
        held[...],
        (((0,), (0,)), ((), ())),
        preferred_element_type=F32,
    )
    out_ref[...] = p_ref[...].T + (more[:rank] + more[rank:])


def left_last(order, hidden, parts, q_turned, p_rest):
    vmem = pl.BlockSpec(memory_space=pltpu.VMEM)
    sources = order.shape[0]
    feats = hidden.shape[1]
    return pl.pallas_call(
        functools.partial(left_kernel, len(parts), sources),
        in_specs=[pl.BlockSpec(memory_space=pltpu.SMEM), pl.BlockSpec(memory_space=pl.ANY)]
        + [vmem] * (len(parts) + 2),
        out_specs=vmem,
        out_shape=jax.ShapeDtypeStruct(p_rest.shape[::-1], F32),
        scratch_shapes=[
            pltpu.VMEM((sources * CAP, feats), BF16),
            pltpu.SemaphoreType.DMA((sources,)),
        ],
        compiler_params=pltpu.CompilerParams(vmem_limit_bytes=16 << 20),
        name="left_last",
    )(order, hidden, *parts, q_turned, p_rest)


def tail_kernel(sources, order, hidden_ref, *refs):
    part_ref, acc_ref, high_ref, low_ref, turned = refs

    @pl.when(pl.program_id(0) == 0)
    def _():
        turn(order, hidden_ref, turned, sources)

    acc = acc_ref[...] + jnp.dot(turned[...], part_ref[...], preferred_element_type=F32)
    high_ref[...], low_ref[...] = split(acc)


def tail(order, hidden, part, acc, tile=256):
    rows, width = acc.shape
    slots, feats = hidden.shape
    sources = order.shape[0]
    flat = pl.BlockSpec((rows, tile), lambda i, order: (0, i))
    return pl.pallas_call(
        functools.partial(tail_kernel, sources),
        grid_spec=pltpu.PrefetchScalarGridSpec(
            num_scalar_prefetch=1,
            grid=(width // tile,),
            in_specs=[pl.BlockSpec((slots, feats), lambda i, order: (0, 0))]
            + [pl.BlockSpec((part.shape[0], tile), lambda i, order: (0, i)), flat],
            out_specs=[flat, flat],
            scratch_shapes=[pltpu.VMEM((feats, sources * CAP), BF16)],
        ),
        out_shape=[jax.ShapeDtypeStruct((rows, width), BF16)] * 2,
        cost_estimate=pl.CostEstimate(
            flops=2 * feats * sources * CAP * width,
            bytes_accessed=rows * width * 8 + sources * CAP * (feats + width) * 2,
            transcendentals=0,
        ),
        compiler_params=pltpu.CompilerParams(vmem_limit_bytes=32 << 20),
        name="tail",
    )(order, hidden, part, acc)


def factors_kernel(a_ref, b_ref, c_ref, d_ref, high_hbm, low_hbm, p_ref, q_ref, high, low, sems):
    copies = [
        pltpu.make_async_copy(high_hbm, high, sems.at[0]),
        pltpu.make_async_copy(low_hbm, low, sems.at[1]),
    ]
    for copy in copies:
        copy.start()
    current = (a_ref[...] + b_ref[...]) + (c_ref[...] + d_ref[...])
    count = current.shape[0]
    row = lax.broadcasted_iota(jnp.int32, (count, 1), 0)
    for i in range(count):
        vector = current[i : i + 1, :]
        dots = jnp.sum(current * vector, axis=1, keepdims=True)
        norm2 = dots[i : i + 1, :]
        coeffs = jnp.where(row > i, dots / norm2, 0.0)
        scale = jnp.where(row == i, lax.rsqrt(norm2), 1.0)
        current = current * scale - coeffs * vector
    p_ref[...] = current
    p_high = current.astype(BF16)
    p_low = (current - p_high.astype(F32)).astype(BF16)
    p_both = jnp.concatenate([p_high, p_low], axis=0)
    for copy in copies:
        copy.wait()
    for c in range(0, q_ref.shape[1], 512):
        both = jnp.dot(p_both, high[:, c : c + 512], preferred_element_type=F32)
        rest = jnp.dot(p_high, low[:, c : c + 512], preferred_element_type=F32)
        q_ref[:, c : c + 512] = both[:count] + (both[count:] + rest)


def factors(parts, high, low):
    rank = parts[0].shape[0]
    rows, width = high.shape
    vmem, far = pl.BlockSpec(memory_space=pltpu.VMEM), pl.BlockSpec(memory_space=pl.ANY)
    return pl.pallas_call(
        factors_kernel,
        in_specs=[vmem] * 4 + [far] * 2,
        out_specs=[vmem] * 2,
        out_shape=[
            jax.ShapeDtypeStruct((rank, rows), F32),
            jax.ShapeDtypeStruct((rank, width), F32),
        ],
        scratch_shapes=[
            pltpu.VMEM((rows, width), BF16),
            pltpu.VMEM((rows, width), BF16),
            pltpu.SemaphoreType.DMA((2,)),
        ],
        compiler_params=pltpu.CompilerParams(vmem_limit_bytes=24 << 20),
        name="factors",
    )(*parts, high, low)


def finish_kernel(p_ref, a_ref, b_ref, c_ref, d_ref, high_ref, low_ref, out_ref, q_ref):
    q = (a_ref[...].astype(F32) + b_ref[...].astype(F32)) + (
        c_ref[...].astype(F32) + d_ref[...].astype(F32)
    )
    q = q * 0.125
    q_ref[...] = q
    q_high = q.astype(BF16)
    q_low = (q - q_high.astype(F32)).astype(BF16)
    p = p_ref[...]
    p_high = p.astype(BF16)
    p_low = (p - p_high.astype(F32)).astype(BF16)
    approx = lax.dot_general(
        jnp.concatenate([p_high, p_high, p_low], axis=0),
        jnp.concatenate([q_high, q_low, q_high], axis=0),
        (((0,), (0,)), ((), ())),
        preferred_element_type=F32,
    )
    acc = high_ref[...].astype(F32) + low_ref[...].astype(F32)
    out_ref[...] = (acc - approx).astype(BF16)


def finish(p_hat, parts, high, low, tile=256):
    rank, rows = p_hat.shape
    width = high.shape[1]
    flat = pl.BlockSpec((rows, tile), lambda i: (0, i))
    thin = pl.BlockSpec((rank, tile), lambda i: (0, i))
    return pl.pallas_call(
        finish_kernel,
        grid=(width // tile,),
        in_specs=[pl.BlockSpec((rank, rows), lambda i: (0, 0))] + [thin] * 4 + [flat] * 2,
        out_specs=[flat, thin],
        out_shape=[
            jax.ShapeDtypeStruct((rows, width), BF16),
            jax.ShapeDtypeStruct((rank, width), F32),
        ],
        compiler_params=pltpu.CompilerParams(vmem_limit_bytes=16 << 20),
        name="finish",
    )(p_hat, *parts, high, low)


def partner(value, k):
    return lax.ppermute(value, "rep", [(i, i ^ k) for i in range(8)])


def body(grad_out, gates, routes, hidden, error, q_init):
    me = lax.axis_index("exp").astype(jnp.int32)
    x, z = me // NZ, me % NZ
    ids = jnp.arange(NX, dtype=jnp.int32) * NZ + z
    own, sent = pack(grad_out[0], routes[0].T, gates[0].T, ids)

    b = {0: own}
    parts, order = [], []
    columns = [[i * NZ + k for i in range(NX)] for k in range(NZ)]

    def spread(group, sent):
        parts.append(
            lax.all_to_all(
                sent, "exp", split_axis=0, concat_axis=0, tiled=True, axis_index_groups=columns
            )
        )
        dx = jnp.array([i for i in range(NX) for k in group], jnp.int32)
        dz = jnp.array([k for i in range(NX) for k in group], jnp.int32)
        order.append(dx * NZ + (z - dz) % NZ)

    b[1] = move(b[0], 0, 1)
    b[7] = move(b[0], 0, -1)
    b[2] = move(b[1], 0, 1)
    b[6] = move(b[7], 0, -1)
    b[3] = move(b[2], 0, 1)
    b[5] = move(b[6], 0, -1)
    b[4] = move(b[3], 0, 1)
    spread(GROUPS[0], sent)
    for group in GROUPS[1:4]:
        spread(group, select([b[k] for k in group], ids))
    held = hidden[0, 0]
    q_turned = jnp.concatenate(split(q_init[0]), axis=0).T
    (acc,) = product(jnp.concatenate(order[:3]), held, parts[:3], error[0, 0])
    spread(GROUPS[4], select([b[k] for k in GROUPS[4]], ids, (acc,)))
    acc, p_rest = product(order[3], held, parts[3:4], acc, q_turned)
    p_local = left_last(order[-1], held, parts[-1:], q_turned, p_rest)
    p_chip = p_local + partner(p_local, 1)
    p_parts = [p_chip] + [partner(p_chip, k) for k in (2, 4, 6)]
    high, low = tail(order[-1], held, parts[-1], acc)
    p_hat, q_local = factors(p_parts, high, low)
    q_chip = (q_local + partner(q_local, 1)).astype(BF16)
    new_error, q_mean = finish(p_hat, [q_chip] + [partner(q_chip, k) for k in (2, 4, 6)], high, low)
    return new_error[None, None], p_hat[None], q_mean[None]


def solution(mesh):
    return jax.shard_map(
        body,
        mesh=mesh,
        in_specs=(
            P("rep", "exp", None),
            P("rep", "exp", None),
            P("rep", "exp", None),
            P("rep", "exp", None, None),
            P("rep", "exp", None, None),
            P("exp", None, None),
        ),
        out_specs=(P("rep", "exp", None, None), P("exp", None, None), P("exp", None, None)),
        check_vma=False,
    )
```

time: 716 us -> 186 us (0.26); the launches traced: 704 us -> 185 us
  waiting for transfers between devices: 314 us -> 59.3 us
  other arithmetic: 217 us -> 1.81 us
  matrix products: 66 us -> 0 us
  Pallas kernels: 0 us -> 48.5 us
  starting transfers between devices: 12.5 us -> 47.3 us
  local copies, waits for them, and re-layouts: 58.5 us -> 27 us
  loops' own time: 22.4 us -> 0 us
  between operations: 14.1 us -> 0.97 us
    all_to_all x1 -> x5, waiting for transfers between devices: 183 us -> 16 us  [spread(): lax.all_to_all(sent, 'exp', split_axis=0, concat_axis=0, tiled=True, axis...]
    psum x2 -> x0, waiting for transfers between devices: 130 us -> none  [the longest x1 67 us: body(): p_total = lax.psum(p_local, 'rep')]
    another operation x67 -> x0, other arithmetic: 76.4 us -> none
    dot_general x36 -> x0, matrix products: 66 us -> none  [the longest x32 33.6 us: step(): coeffs = jnp.dot(current, vector, precision=lax.Precision.HIGHEST)]
    sub x32 -> x0, other arithmetic: 52.6 us -> none  [step(): current - jnp.where(index > i, coeffs, 0.0)[:, None] * vector[None, :]]
    pallas_call x0 -> x11, Pallas kernels: none -> 48.5 us  [the longest x2 21.5 us: product(): pl.pallas_call(functools.partial(kernel, len(parts), sources), grid_spec=...]
    reduce_sum x33 -> x0, other arithmetic: 44.6 us -> none  [the longest x32 44.5 us: step(): vector = vector / jnp.sqrt(jnp.sum(vector * vector))]
    scatter x32 -> x0, local copies, waits for them, and re-layouts: 43.4 us -> none  [step(): return current.at[i].set(vector)]
  transfers between devices with their start and end apart: 3 -> 20, of which waited for: 3 -> 11; matrix products, arithmetic and copies ran while one was open for 1% -> 2% of each run, Pallas kernels for 0% -> 18%
where the time goes in v1:
time: 186 us; the launch traced here: 185 us
  waiting for transfers between devices  59.3 us (32%)
  Pallas kernels  48.5 us (26%)
  starting transfers between devices  47.3 us (25%)
  local copies, waits for them, and re-layouts  27 us (15%)
    ppermute x7, waiting for transfers between devices, move(): return lax.ppermute(block, 'exp', pairs)  32.6 us
    unnamed x53, local copies, waits for them, and re-layouts  27 us
    all_to_all x5, starting transfers between devices, spread(): lax.all_to_all(sent, 'exp', split_axis=0, concat_axis=0, tiled=True, axis...  22.1 us
    pallas_call x2, Pallas kernels, product(): pl.pallas_call(functools.partial(kernel, len(parts), sources), grid_spec=...  21.5 us
    all_to_all x5, waiting for transfers between devices, spread(): lax.all_to_all(sent, 'exp', split_axis=0, concat_axis=0, tiled=True, axis...  16 us
    ppermute x8, starting transfers between devices, partner(): return lax.ppermute(value, 'rep', [(i, i ^ k) for i in range(8)])  14.2 us
    ppermute x7, starting transfers between devices, move(): return lax.ppermute(block, 'exp', pairs)  11.1 us
    ppermute x8, waiting for transfers between devices, partner(): return lax.ppermute(value, 'rep', [(i, i ^ k) for i in range(8)])  10.7 us
  transfers between devices with their start and end apart: 20, of which 11 were waited for; matrix products, arithmetic and copies ran while one was open for 2% of the time, Pallas kernels for 18%

profile of v1, /device:TPU:1, one launch (start us, length us, event | category | flops | bytes accessed | tf_op | source)
XLA Modules:
  0.0 184.9 jit_solution(15367550931019212285)
XLA Ops:
  0.7 1.0 copy-done.17
  3.1 2.1 %pack.1 = (bf16[136,2048]{1,0:T(8,128)(2,1)S(1)}, bf16[256,2048]{1,0:T(8,128)(2,1)}) custom-call(s32[4]{0:T(128)S(1)} %fusion.7.ids_ref, bf16[128,2048]{1,0:T(8,128)(2,1)S(1)} %bitcast.41, s32[8,128]{1,0:T(8,128)S(1)} %bitcast.43, f32[8,128]{1,0:T(8,128)S(1)} %bitcast.44), custom_call_target="tpu_custom_call" | custom-call | bytes 2097152 | tf_op jit(solution)/shard_map/pack/pallas_call | solution.py:107
  5.2 4.8 %all-to-all-start = ((bf16[4,64,2048]{2,1,0:T(8,128)(2,1)}), bf16[4,64,2048]{2,1,0:T(8,128)(2,1)S(1)}, u32[]{:S(2)}, u32[]{:S(2)}) async-start(bf16[4,64,2048]{2,1,0:T(8,128)(2,1)} %bitcast.6), calls=%async_computation | async-start | bytes 2097152 | tf_op jit(solution)/shard_map/all_to_all | solution.py:403
  10.0 1.6 collective-permute-start
  11.7 3.9 %collective-permute-start.4 = (bf16[136,2048]{1,0:T(8,128)(2,1)S(1)}, bf16[136,2048]{1,0:T(8,128)(2,1)S(1)}, u32[]{:S(2)}, u32[]{:S(2)}) collective-permute-start(bf16[136,2048]{1,0:T(8,128)(2,1)S(1)} %get-tuple-element.13), channel_id=1, source_target_pairs={{0,7},{1,0},{2,1},{3,2},{4,3},{5,4},{6,5},{7,6},{8,15},{9,8},{10,9... | collective-permute-start | bytes 1671176 | tf_op jit(solution)/shard_map/ppermute | solution.py:26
  15.6 12.1 %collective-permute-done.refs_0_ = bf16[136,2048]{1,0:T(8,128)(2,1)} collective-permute-done((bf16[136,2048]{1,0:T(8,128)(2,1)S(1)}, bf16[136,2048]{1,0:T(8,128)(2,1)}, u32[]{:S(2)}, u32[]{:S(2)}) %collective-permute-start) | collective-permute-done | bytes 557088 | tf_op jit(solution)/shard_map/ppermute | solution.py:26
  27.7 2.0 %select.16 = bf16[512,2048]{1,0:T(8,128)(2,1)S(1)} custom-call(s32[4]{0:T(128)S(1)} %fusion.7.ids_ref, bf16[136,2048]{1,0:T(8,128)(2,1)} %collective-permute-done.refs_0_, bf16[136,2048]{1,0:T(8,128)(2,1)S(1)} %collective-permute-done.4.refs_1_), custom_call_target="tpu_custom_call" | custom-call | flops 268435456 | bytes 3211264 | tf_op jit(solution)/shard_map/select/pallas_call | solution.py:73
  29.8 1.3 copy-done.6
  31.9 1.0 copy-done.11
  32.9 3.9 %all-to-all-start.1 = ((bf16[4,128,2048]{2,1,0:T(8,128)(2,1)}), bf16[4,128,2048]{2,1,0:T(8,128)(2,1)S(1)}, u32[]{:S(2)}, u32[]{:S(2)}) async-start(bf16[4,128,2048]{2,1,0:T(8,128)(2,1)} %bitcast.37), calls=%async_computation.1 | async-start | bytes 4194304 | tf_op jit(solution)/shard_map/all_to_all | solution.py:403
  36.8 2.7 %collective-permute-start.5 = (bf16[136,2048]{1,0:T(8,128)(2,1)}, bf16[136,2048]{1,0:T(8,128)(2,1)S(1)}, u32[]{:S(2)}, u32[]{:S(2)}) collective-permute-start(bf16[136,2048]{1,0:T(8,128)(2,1)} %copy-done.16), channel_id=1, source_target_pairs={{0,7},{1,0},{2,1},{3,2},{4,3},{5,4},{6,5},{7,6},{8,15},{9,8},{10,9... | collective-permute-start | bytes 1671176 | tf_op jit(solution)/shard_map/ppermute | solution.py:26
  39.5 10.7 %collective-permute-done.1.refs_0_ = bf16[136,2048]{1,0:T(8,128)(2,1)S(1)} collective-permute-done((bf16[136,2048]{1,0:T(8,128)(2,1)}, bf16[136,2048]{1,0:T(8,128)(2,1)S(1)}, u32[]{:S(2)}, u32[]{:S(2)}) %collective-permute-start.1) | collective-permute-done | bytes 557088 | tf_op jit(solution)/shard_map/ppermute | solution.py:26
  50.2 1.5 select.17
  51.7 1.3 copy-done.5
  53.1 8.0 %all-to-all-done.1 = bf16[4,128,2048]{2,1,0:T(8,128)(2,1)S(1)} async-done(((bf16[4,128,2048]{2,1,0:T(8,128)(2,1)}), bf16[4,128,2048]{2,1,0:T(8,128)(2,1)S(1)}, u32[]{:S(2)}, u32[]{:S(2)}) %all-to-all-start.1) | async-done | bytes 2097184 | tf_op jit(solution)/shard_map/all_to_all | solution.py:403
  61.0 4.4 %all-to-all-start.2 = ((bf16[4,128,2048]{2,1,0:T(8,128)(2,1)}), bf16[4,128,2048]{2,1,0:T(8,128)(2,1)}, u32[]{:S(2)}, u32[]{:S(2)}) async-start(bf16[4,128,2048]{2,1,0:T(8,128)(2,1)} %bitcast.36), calls=%async_computation.2 | async-start | bytes 4194304 | tf_op jit(solution)/shard_map/all_to_all | solution.py:403
  65.6 2.7 %collective-permute-start.6 = (bf16[136,2048]{1,0:T(8,128)(2,1)S(1)}, bf16[136,2048]{1,0:T(8,128)(2,1)S(1)}, u32[]{:S(2)}, u32[]{:S(2)}) collective-permute-start(bf16[136,2048]{1,0:T(8,128)(2,1)S(1)} %collective-permute-done.5.refs_1_), channel_id=1, source_target_pairs={{0,7},{1,0},{2,1},{3,2},{4,3},{5,4},{6,5},{7,6},{8,15},{9,8},{10,9... | collective-permute-start | bytes 1671176 | tf_op jit(solution)/shard_map/ppermute | solution.py:26
  68.3 9.7 %collective-permute-done.2.refs_0_ = bf16[136,2048]{1,0:T(8,128)(2,1)S(1)} collective-permute-done((bf16[136,2048]{1,0:T(8,128)(2,1)S(1)}, bf16[136,2048]{1,0:T(8,128)(2,1)S(1)}, u32[]{:S(2)}, u32[]{:S(2)}) %collective-permute-start.2) | collective-permute-done | bytes 557088 | tf_op jit(solution)/shard_map/ppermute | solution.py:26
  78.0 1.5 select.19
  79.5 1.3 copy-done.4
  81.6 7.2 %all-to-all-done.2 = bf16[4,128,2048]{2,1,0:T(8,128)(2,1)} async-done(((bf16[4,128,2048]{2,1,0:T(8,128)(2,1)}), bf16[4,128,2048]{2,1,0:T(8,128)(2,1)}, u32[]{:S(2)}, u32[]{:S(2)}) %all-to-all-start.2) | async-done | bytes 2097184 | tf_op jit(solution)/shard_map/all_to_all | solution.py:403
  88.9 4.4 %all-to-all-start.4 = ((bf16[4,128,2048]{2,1,0:T(8,128)(2,1)}), bf16[4,128,2048]{2,1,0:T(8,128)(2,1)}, u32[]{:S(2)}, u32[]{:S(2)}) async-start(bf16[4,128,2048]{2,1,0:T(8,128)(2,1)} %bitcast.35), calls=%async_computation.4 | async-start | bytes 4194304 | tf_op jit(solution)/shard_map/all_to_all | solution.py:403
  93.4 1.3 copy.19
  94.9 1.6 copy-done.3
  96.5 1.2 copy-done.12
  97.7 1.9 %copy-done.14 = bf16[1,1,768,2048]{3,2,1,0:T(8,128)(2,1)S(1)} copy-done((bf16[1,1,768,2048]{3,2,1,0:T(8,128)(2,1)S(1)}, bf16[1,1,768,2048]{3,2,1,0:T(8,128)(2,1)}, u32[]{:S(2)}) %copy-start.14) | copy-done | bytes 3145752
  99.6 10.4 %product.2.refs_1_ = f32[768,2048]{1,0:T(8,128)} custom-call(s32[20]{0:T(128)S(1)} %pad_add_fusion.order, bf16[2048,768]{1,0:T(8,128)(2,1)S(1)} %bitcast.30, bf16[256,2048]{1,0:T(8,128)(2,1)S(1)} %bitcast.38, bf16[512,2048]{1,0:T(8,128)(2,1)S(1)} %bitcast.34, bf16[512,2048]{1,0:T(8,128)(2,1)} %bitcast.11.refs_2_, bf16[768,2048]{1,0:T(8,128)(2,1)S(1)} %bitcast.40), custom_call_target="tpu_custom_call" | custom-call | flops 4026531840 | bytes 19791872 | tf_op jit(solution)/shard_map/product/pallas_call | solution.py:192
  110.1 2.8 %copy-done = f32[768,2048]{1,0:T(8,128)S(1)} copy-done((f32[768,2048]{1,0:T(8,128)S(1)}, f32[768,2048]{1,0:T(8,128)}, u32[]{:S(2)}) %copy-start) | copy-done | bytes 6291480
  112.8 1.1 select.18
  114.0 1.0 copy-done.13
  115.8 4.4 %all-to-all-start.3 = ((bf16[4,64,2048]{2,1,0:T(8,128)(2,1)}), bf16[4,64,2048]{2,1,0:T(8,128)(2,1)}, u32[]{:S(2)}, u32[]{:S(2)}) async-start(bf16[4,64,2048]{2,1,0:T(8,128)(2,1)} %bitcast.39), calls=%async_computation.3 | async-start | bytes 2097152 | tf_op jit(solution)/shard_map/all_to_all | solution.py:403
  120.2 1.4 fusion
  121.9 11.1 %product.3 = (f32[768,2048]{1,0:T(8,128)S(1)}, f32[768,32]{1,0:T(8,128)S(1)}) custom-call(s32[8]{0:T(128)S(1)} %get-tuple-element.25.order, bf16[2048,768]{1,0:T(8,128)(2,1)S(1)} %bitcast.31, bf16[512,2048]{1,0:T(8,128)(2,1)} %bitcast.18.refs_0_, f32[768,2048]{1,0:T(8,128)} %product.2.refs_1_, bf16[2048,64]{1,0:T(8,128)(2,1)S(1)} %maximum_bitcast_fusion.refs_2_.refs_1_), custom_call_target="tpu_custom_call" | custom-call | flops 1610612736 | bytes 15466496 | tf_op jit(solution)/shard_map/product/pallas_call | solution.py:192
  133.0 2.7 %copy-done.7 = f32[768,2048]{1,0:T(8,128)} copy-done((f32[768,2048]{1,0:T(8,128)}, f32[768,2048]{1,0:T(8,128)S(1)}, u32[]{:S(2)}) %copy-start.7) | copy-done | bytes 6291480
  136.5 1.0 copy-done.10
  137.5 2.6 %left_last.1 = f32[32,768]{1,0:T(8,128)S(1)} custom-call(s32[4]{0:T(128)S(1)} %fusion.9.order, bf16[2048,768]{1,0:T(8,128)(2,1)S(1)} %bitcast.32, bf16[256,2048]{1,0:T(8,128)(2,1)} %bitcast.14.refs_0_, bf16[2048,64]{1,0:T(8,128)(2,1)S(1)} %copy-done.10, f32[768,32]{1,0:T(8,128)S(1)} %get-tuple-element.15.refs_2_), custom_call_target="tpu_custom_call" | custom-call | tf_op jit(solution)/shard_map/left_last/pallas_call | solution.py:244
  140.1 5.0 %collective-permute-start.7 = (f32[32,768]{1,0:T(8,128)S(1)}, f32[32,768]{1,0:T(8,128)S(1)}, u32[]{:S(2)}, u32[]{:S(2)}) collective-permute-start(f32[32,768]{1,0:T(8,128)S(1)} %left_last.1), channel_id=1, source_target_pairs={{0,32},{32,0},{64,96},{96,64},{128,160},{160,128},{192,224},{224,1... | collective-permute-start | bytes 294920 | tf_op jit(solution)/shard_map/ppermute | solution.py:388
  146.1 2.8 %collective-permute-start.10 = (f32[32,768]{1,0:T(8,128)S(1)}, f32[32,768]{1,0:T(8,128)S(1)}, u32[]{:S(2)}, u32[]{:S(2)}) collective-permute-start(f32[32,768]{1,0:T(8,128)S(1)} %add.65.a_ref), channel_id=1, source_target_pairs={{0,192},{32,224},{64,128},{96,160},{128,64},{160,96},{192,0},{224,... | collective-permute-start | bytes 294920 | tf_op jit(solution)/shard_map/ppermute | solution.py:388
  148.9 1.3 collective-permute-start.9
  150.1 2.8 %copy-done.8 = f32[768,2048]{1,0:T(8,128)S(1)} copy-done((f32[768,2048]{1,0:T(8,128)S(1)}, f32[768,2048]{1,0:T(8,128)}, u32[]{:S(2)}) %copy-start.8) | copy-done | bytes 6291480
  152.9 6.4 %tail.1 = (bf16[768,2048]{1,0:T(8,128)(2,1)S(1)}, bf16[768,2048]{1,0:T(8,128)(2,1)S(1)}) custom-call(s32[4]{0:T(128)S(1)} %fusion.9.order, bf16[2048,768]{1,0:T(8,128)(2,1)S(1)} %bitcast.33, bf16[256,2048]{1,0:T(8,128)(2,1)} %bitcast.14.refs_0_, f32[768,2048]{1,0:T(8,128)S(1)} %copy-done.8), custom_call_target="tpu_custom_call" | custom-call | flops 805306368 | bytes 14024704 | tf_op jit(solution)/shard_map/tail/pallas_call | solution.py:275
  159.4 4.7 %factors.1 = (f32[32,768]{1,0:T(8,128)}, f32[32,2048]{1,0:T(8,128)S(1)}) custom-call(f32[32,768]{1,0:T(8,128)S(1)} %add.65.a_ref, f32[32,768]{1,0:T(8,128)S(1)} %collective-permute-done.8.b_ref, f32[32,768]{1,0:T(8,128)S(1)} %collective-permute-done.9.c_ref, f32[32,768]{1,0:T(8,128)S(1)} %collective-permute-done.10.d_ref, ...), custom_call_target="tpu_custom_call" | custom-call | tf_op jit(solution)/shard_map/factors/pallas_call | solution.py:329
  164.0 1.1 collective-permute-start.11
  165.2 1.2 collective-permute-done.11
  166.5 3.8 %collective-permute-start.13 = (bf16[32,2048]{1,0:T(8,128)(2,1)S(1)}, bf16[32,2048]{1,0:T(8,128)(2,1)S(1)}, u32[]{:S(2)}, u32[]{:S(2)}) collective-permute-start(bf16[32,2048]{1,0:T(8,128)(2,1)S(1)} %add_convert_fusion.a_ref), channel_id=1, source_target_pairs={{0,128},{32,160},{64,192},{96,224},{128,0},{160,32},{192,64},{224,... | collective-permute-start | bytes 393224 | tf_op jit(solution)/shard_map/ppermute | solution.py:388
  171.2 5.3 %collective-permute-done.13.c_ref = bf16[32,2048]{1,0:T(8,128)(2,1)S(1)} collective-permute-done((bf16[32,2048]{1,0:T(8,128)(2,1)S(1)}, bf16[32,2048]{1,0:T(8,128)(2,1)S(1)}, u32[]{:S(2)}, u32[]{:S(2)}) %collective-permute-start.13) | collective-permute-done | bytes 131104 | tf_op jit(solution)/shard_map/ppermute | solution.py:388
  176.4 2.5 %collective-permute-done.14.d_ref = bf16[32,2048]{1,0:T(8,128)(2,1)S(1)} collective-permute-done((bf16[32,2048]{1,0:T(8,128)(2,1)S(1)}, bf16[32,2048]{1,0:T(8,128)(2,1)S(1)}, u32[]{:S(2)}, u32[]{:S(2)}) %collective-permute-start.14) | collective-permute-done | bytes 131104 | tf_op jit(solution)/shard_map/ppermute | solution.py:388
  179.8 5.1 %finish.1 = (bf16[768,2048]{1,0:T(8,128)(2,1)}, f32[32,2048]{1,0:T(8,128)}) custom-call(f32[32,768]{1,0:T(8,128)S(1)} %copy-done.18, bf16[32,2048]{1,0:T(8,128)(2,1)S(1)} %add_convert_fusion.a_ref, bf16[32,2048]{1,0:T(8,128)(2,1)S(1)} %collective-permute-done.12.b_ref, bf16[32,2048]{1,0:T(8,128)(2,1)S(1)} %collective-permute-done.13.c_ref, ...), custom_call_target="tpu_custom_call" | custom-call | tf_op jit(solution)/shard_map/finish/pallas_call | solution.py:373
  (65 shorter events, 8.1 us)
Async XLA Ops:
  0.7 1.0 copy-start.17
  1.7 0.7 copy-start.19
  2.4 0.7 copy-start.20
  5.2 26.7 %all-to-all-start = ((bf16[4,64,2048]{2,1,0:T(8,128)(2,1)}), bf16[4,64,2048]{2,1,0:T(8,128)(2,1)S(1)}, u32[]{:S(2)}, u32[]{:S(2)}) async-start(bf16[4,64,2048]{2,1,0:T(8,128)(2,1)} %bitcast.6), calls=%async_computation | async-start | bytes 2097152 | tf_op jit(solution)/shard_map/all_to_all | solution.py:403
  10.0 17.7 %collective-permute-start = (bf16[136,2048]{1,0:T(8,128)(2,1)S(1)}, bf16[136,2048]{1,0:T(8,128)(2,1)}, u32[]{:S(2)}, u32[]{:S(2)}) collective-permute-start(bf16[136,2048]{1,0:T(8,128)(2,1)S(1)} %get-tuple-element.13), channel_id=1, source_target_pairs={{0,1},{1,2},{2,3},{3,4},{4,5},{5,6},{6,7},{7,0},{8,9},{9,10},{10,1... | collective-permute-start | bytes 1671176 | tf_op jit(solution)/shard_map/ppermute | solution.py:26
  11.7 16.1 %collective-permute-start.4 = (bf16[136,2048]{1,0:T(8,128)(2,1)S(1)}, bf16[136,2048]{1,0:T(8,128)(2,1)S(1)}, u32[]{:S(2)}, u32[]{:S(2)}) collective-permute-start(bf16[136,2048]{1,0:T(8,128)(2,1)S(1)} %get-tuple-element.13), channel_id=1, source_target_pairs={{0,7},{1,0},{2,1},{3,2},{4,3},{5,4},{6,5},{7,6},{8,15},{9,8},{10,9... | collective-permute-start | bytes 1671176 | tf_op jit(solution)/shard_map/ppermute | solution.py:26
  29.8 1.3 copy-start.6
  31.1 0.8 copy-start.16
  31.9 1.0 copy-start.11
  32.9 28.2 %all-to-all-start.1 = ((bf16[4,128,2048]{2,1,0:T(8,128)(2,1)}), bf16[4,128,2048]{2,1,0:T(8,128)(2,1)S(1)}, u32[]{:S(2)}, u32[]{:S(2)}) async-start(bf16[4,128,2048]{2,1,0:T(8,128)(2,1)} %bitcast.37), calls=%async_computation.1 | async-start | bytes 4194304 | tf_op jit(solution)/shard_map/all_to_all | solution.py:403
  36.8 13.4 %collective-permute-start.1 = (bf16[136,2048]{1,0:T(8,128)(2,1)}, bf16[136,2048]{1,0:T(8,128)(2,1)S(1)}, u32[]{:S(2)}, u32[]{:S(2)}) collective-permute-start(bf16[136,2048]{1,0:T(8,128)(2,1)} %collective-permute-done.refs_0_), channel_id=1, source_target_pairs={{0,1},{1,2},{2,3},{3,4},{4,5},{5,6},{6,7},{7,0},{8,9},{9,10},{10,1... | collective-permute-start | bytes 1671176 | tf_op jit(solution)/shard_map/ppermute | solution.py:26
  36.8 13.4 %collective-permute-start.5 = (bf16[136,2048]{1,0:T(8,128)(2,1)}, bf16[136,2048]{1,0:T(8,128)(2,1)S(1)}, u32[]{:S(2)}, u32[]{:S(2)}) collective-permute-start(bf16[136,2048]{1,0:T(8,128)(2,1)} %copy-done.16), channel_id=1, source_target_pairs={{0,7},{1,0},{2,1},{3,2},{4,3},{5,4},{6,5},{7,6},{8,15},{9,8},{10,9... | collective-permute-start | bytes 1671176 | tf_op jit(solution)/shard_map/ppermute | solution.py:26
  51.7 1.3 copy-start.5
  61.0 16.9 %copy-start.2 = (bf16[4,128,2048]{2,1,0:T(8,128)(2,1)}, bf16[4,128,2048]{2,1,0:T(8,128)(2,1)S(1)}, u32[]{:S(2)}) copy-start(bf16[4,128,2048]{2,1,0:T(8,128)(2,1)S(1)} %all-to-all-done.1) | copy-start | bytes 6291460
  61.0 27.8 %all-to-all-start.2 = ((bf16[4,128,2048]{2,1,0:T(8,128)(2,1)}), bf16[4,128,2048]{2,1,0:T(8,128)(2,1)}, u32[]{:S(2)}, u32[]{:S(2)}) async-start(bf16[4,128,2048]{2,1,0:T(8,128)(2,1)} %bitcast.36), calls=%async_computation.2 | async-start | bytes 4194304 | tf_op jit(solution)/shard_map/all_to_all | solution.py:403
  65.5 27.9 %copy-start.21 = (f32[1,32,2048]{2,1,0:T(8,128)S(1)}, f32[1,32,2048]{2,1,0:T(8,128)}, u32[]{:S(2)}) copy-start(f32[1,32,2048]{2,1,0:T(8,128)} %param.21) | copy-start | bytes 786436
  65.5 12.5 %collective-permute-start.2 = (bf16[136,2048]{1,0:T(8,128)(2,1)S(1)}, bf16[136,2048]{1,0:T(8,128)(2,1)S(1)}, u32[]{:S(2)}, u32[]{:S(2)}) collective-permute-start(bf16[136,2048]{1,0:T(8,128)(2,1)S(1)} %collective-permute-done.1.refs_0_), channel_id=1, source_target_pairs={{0,1},{1,2},{2,3},{3,4},{4,5},{5,6},{6,7},{7,0},{8,9},{9,10},{10,1... | collective-permute-start | bytes 1671176 | tf_op jit(solution)/shard_map/ppermute | solution.py:26
  65.6 12.4 %collective-permute-start.6 = (bf16[136,2048]{1,0:T(8,128)(2,1)S(1)}, bf16[136,2048]{1,0:T(8,128)(2,1)S(1)}, u32[]{:S(2)}, u32[]{:S(2)}) collective-permute-start(bf16[136,2048]{1,0:T(8,128)(2,1)S(1)} %collective-permute-done.5.refs_1_), channel_id=1, source_target_pairs={{0,7},{1,0},{2,1},{3,2},{4,3},{5,4},{6,5},{7,6},{8,15},{9,8},{10,9... | collective-permute-start | bytes 1671176 | tf_op jit(solution)/shard_map/ppermute | solution.py:26
  79.5 1.3 copy-start.4
  80.8 0.8 copy-start.15
  81.6 13.1 %copy-start.22 = (s32[8]{0:T(128)S(1)}, s32[8]{0:T(128)}, u32[]{:S(2)}) copy-start(s32[8]{0:T(128)} %constant.77) | copy-start | bytes 100
  81.6 13.1 %copy-start.23 = (s32[8]{0:T(128)S(1)}, s32[8]{0:T(128)}, u32[]{:S(2)}) copy-start(s32[8]{0:T(128)} %constant.78) | copy-start | bytes 100
  81.6 13.1 %copy-start.24 = (s32[8]{0:T(128)S(1)}, s32[8]{0:T(128)}, u32[]{:S(2)}) copy-start(s32[8]{0:T(128)} %constant.79) | copy-start | bytes 100
  81.6 13.1 %copy-start.25 = (s32[8]{0:T(128)S(1)}, s32[8]{0:T(128)}, u32[]{:S(2)}) copy-start(s32[8]{0:T(128)} %constant.80) | copy-start | bytes 100
  81.6 13.3 %copy-start.1 = (bf16[1,1,2048,768]{3,2,1,0:T(8,128)(2,1)S(1)}, bf16[1,1,2048,768]{3,2,1,0:T(8,128)(2,1)}, u32[]{:S(2)}) copy-start(bf16[1,1,2048,768]{3,2,1,0:T(8,128)(2,1)} %param.19) | copy-start | bytes 9437188
  88.9 26.9 %all-to-all-start.4 = ((bf16[4,128,2048]{2,1,0:T(8,128)(2,1)}), bf16[4,128,2048]{2,1,0:T(8,128)(2,1)}, u32[]{:S(2)}, u32[]{:S(2)}) async-start(bf16[4,128,2048]{2,1,0:T(8,128)(2,1)} %bitcast.35), calls=%async_computation.4 | async-start | bytes 4194304 | tf_op jit(solution)/shard_map/all_to_all | solution.py:403
  94.7 15.3 %collective-permute-start.3 = (bf16[136,2048]{1,0:T(8,128)(2,1)}, bf16[136,2048]{1,0:T(8,128)(2,1)S(1)}, u32[]{:S(2)}, u32[]{:S(2)}) collective-permute-start(bf16[136,2048]{1,0:T(8,128)(2,1)} %copy-done.15), channel_id=1, source_target_pairs={{0,1},{1,2},{2,3},{3,4},{4,5},{5,6},{6,7},{7,0},{8,9},{9,10},{10,1... | collective-permute-start | bytes 1671176 | tf_op jit(solution)/shard_map/ppermute | solution.py:26
  94.9 1.6 copy-start.3
  96.5 1.2 copy-start.12
  97.7 1.9 %copy-start.14 = (bf16[1,1,768,2048]{3,2,1,0:T(8,128)(2,1)S(1)}, bf16[1,1,768,2048]{3,2,1,0:T(8,128)(2,1)}, u32[]{:S(2)}) copy-start(bf16[1,1,768,2048]{3,2,1,0:T(8,128)(2,1)} %param.20) | copy-start | bytes 9437188
  110.1 2.8 %copy-start = (f32[768,2048]{1,0:T(8,128)S(1)}, f32[768,2048]{1,0:T(8,128)}, u32[]{:S(2)}) copy-start(f32[768,2048]{1,0:T(8,128)} %product.2.refs_1_) | copy-start | bytes 18874372
  114.0 1.0 copy-start.13
  115.8 20.7 %all-to-all-start.3 = ((bf16[4,64,2048]{2,1,0:T(8,128)(2,1)}), bf16[4,64,2048]{2,1,0:T(8,128)(2,1)}, u32[]{:S(2)}, u32[]{:S(2)}) async-start(bf16[4,64,2048]{2,1,0:T(8,128)(2,1)} %bitcast.39), calls=%async_computation.3 | async-start | bytes 2097152 | tf_op jit(solution)/shard_map/all_to_all | solution.py:403
  133.0 2.7 %copy-start.7 = (f32[768,2048]{1,0:T(8,128)}, f32[768,2048]{1,0:T(8,128)S(1)}, u32[]{:S(2)}) copy-start(f32[768,2048]{1,0:T(8,128)S(1)} %get-tuple-element.16.refs_1_) | copy-start | bytes 18874372
  135.7 0.8 copy-start.9
  136.5 1.0 copy-start.10
  140.1 5.9 %collective-permute-start.7 = (f32[32,768]{1,0:T(8,128)S(1)}, f32[32,768]{1,0:T(8,128)S(1)}, u32[]{:S(2)}, u32[]{:S(2)}) collective-permute-start(f32[32,768]{1,0:T(8,128)S(1)} %left_last.1), channel_id=1, source_target_pairs={{0,32},{32,0},{64,96},{96,64},{128,160},{160,128},{192,224},{224,1... | collective-permute-start | bytes 294920 | tf_op jit(solution)/shard_map/ppermute | solution.py:388
  146.1 13.3 %collective-permute-start.10 = (f32[32,768]{1,0:T(8,128)S(1)}, f32[32,768]{1,0:T(8,128)S(1)}, u32[]{:S(2)}, u32[]{:S(2)}) collective-permute-start(f32[32,768]{1,0:T(8,128)S(1)} %add.65.a_ref), channel_id=1, source_target_pairs={{0,192},{32,224},{64,128},{96,160},{128,64},{160,96},{192,0},{224,... | collective-permute-start | bytes 294920 | tf_op jit(solution)/shard_map/ppermute | solution.py:388
  148.9 10.5 %collective-permute-start.8 = (f32[32,768]{1,0:T(8,128)S(1)}, f32[32,768]{1,0:T(8,128)S(1)}, u32[]{:S(2)}, u32[]{:S(2)}) collective-permute-start(f32[32,768]{1,0:T(8,128)S(1)} %add.65.a_ref), channel_id=1, source_target_pairs={{0,64},{32,96},{64,0},{96,32},{128,192},{160,224},{192,128},{224,1... | collective-permute-start | bytes 294920 | tf_op jit(solution)/shard_map/ppermute | solution.py:388
  148.9 10.5 %collective-permute-start.9 = (f32[32,768]{1,0:T(8,128)S(1)}, f32[32,768]{1,0:T(8,128)S(1)}, u32[]{:S(2)}, u32[]{:S(2)}) collective-permute-start(f32[32,768]{1,0:T(8,128)S(1)} %add.65.a_ref), channel_id=1, source_target_pairs={{0,128},{32,160},{64,192},{96,224},{128,0},{160,32},{192,64},{224,... | collective-permute-start | bytes 294920 | tf_op jit(solution)/shard_map/ppermute | solution.py:388
  150.1 2.8 %copy-start.8 = (f32[768,2048]{1,0:T(8,128)S(1)}, f32[768,2048]{1,0:T(8,128)}, u32[]{:S(2)}) copy-start(f32[768,2048]{1,0:T(8,128)} %copy-done.7) | copy-start | bytes 18874372
  164.0 2.3 %collective-permute-start.11 = (f32[32,2048]{1,0:T(8,128)S(1)}, f32[32,2048]{1,0:T(8,128)S(1)}, u32[]{:S(2)}, u32[]{:S(2)}) collective-permute-start(f32[32,2048]{1,0:T(8,128)S(1)} %get-tuple-element.20), channel_id=1, source_target_pairs={{0,32},{32,0},{64,96},{96,64},{128,160},{160,128},{192,224},{224,1... | collective-permute-start | bytes 786440 | tf_op jit(solution)/shard_map/ppermute | solution.py:388
  166.4 4.8 %collective-permute-start.12 = (bf16[32,2048]{1,0:T(8,128)(2,1)S(1)}, bf16[32,2048]{1,0:T(8,128)(2,1)S(1)}, u32[]{:S(2)}, u32[]{:S(2)}) collective-permute-start(bf16[32,2048]{1,0:T(8,128)(2,1)S(1)} %add_convert_fusion.a_ref), channel_id=1, source_target_pairs={{0,64},{32,96},{64,0},{96,32},{128,192},{160,224},{192,128},{224,1... | collective-permute-start | bytes 393224 | tf_op jit(solution)/shard_map/ppermute | solution.py:388
  166.5 9.9 %collective-permute-start.13 = (bf16[32,2048]{1,0:T(8,128)(2,1)S(1)}, bf16[32,2048]{1,0:T(8,128)(2,1)S(1)}, u32[]{:S(2)}, u32[]{:S(2)}) collective-permute-start(bf16[32,2048]{1,0:T(8,128)(2,1)S(1)} %add_convert_fusion.a_ref), channel_id=1, source_target_pairs={{0,128},{32,160},{64,192},{96,224},{128,0},{160,32},{192,64},{224,... | collective-permute-start | bytes 393224 | tf_op jit(solution)/shard_map/ppermute | solution.py:388
  170.3 8.6 %collective-permute-start.14 = (bf16[32,2048]{1,0:T(8,128)(2,1)S(1)}, bf16[32,2048]{1,0:T(8,128)(2,1)S(1)}, u32[]{:S(2)}, u32[]{:S(2)}) collective-permute-start(bf16[32,2048]{1,0:T(8,128)(2,1)S(1)} %add_convert_fusion.a_ref), channel_id=1, source_target_pairs={{0,192},{32,224},{64,128},{96,160},{128,64},{160,96},{192,0},{224,... | collective-permute-start | bytes 393224 | tf_op jit(solution)/shard_map/ppermute | solution.py:388
  178.9 0.9 copy-start.18

commit v2 on v1

--- a/solution.py
+++ b/solution.py
@@ -87,7 +87,7 @@
     )(ids, *blocks, *after)
 
 
-def pack_kernel(experts, ids_ref, grad_ref, routes_ref, gates_ref, block_ref, out_ref):
+def pack_kernel(grad_ref, routes_ref, gates_ref, block_ref):
     gates = gates_ref[...]
     high = gates.astype(BF16)
     rest = gates - high.astype(F32)
@@ -97,25 +97,15 @@
     block_ref[0:TOK, :] = grad_ref[...]
     block_ref[TOK:ROWS, 0 : 4 * TOK] = meta
     block_ref[TOK:ROWS, 4 * TOK :] = jnp.zeros((META, grad_ref.shape[1] - 4 * TOK), BF16)
-    select_kernel((1,), experts, ids_ref, block_ref, out_ref)
-
-
-def pack(grad, routes, gates, ids):
-    vmem = pl.BlockSpec(memory_space=pltpu.VMEM)
-    width = grad.shape[1]
-    experts = ids.shape[0]
-    return pl.pallas_call(
-        functools.partial(pack_kernel, experts),
-        in_specs=[pl.BlockSpec(memory_space=pltpu.SMEM)] + [vmem] * 3,
-        out_specs=[vmem] * 2,
-        out_shape=[
-            jax.ShapeDtypeStruct((ROWS, width), BF16),
-            jax.ShapeDtypeStruct((experts * CAP, width), BF16),
-        ],
-        cost_estimate=pl.CostEstimate(flops=0, bytes_accessed=2 << 20, transcendentals=0),
-        compiler_params=pltpu.CompilerParams(vmem_limit_bytes=32 << 20),
+
+
+def pack(grad, routes, gates):
+    return pl.pallas_call(
+        pack_kernel,
+        out_shape=jax.ShapeDtypeStruct((ROWS, grad.shape[1]), BF16),
+        cost_estimate=pl.CostEstimate(flops=0, bytes_accessed=1 << 20, transcendentals=0),
         name="pack",
-    )(ids, grad, routes, gates)
+    )(grad, routes, gates)
 
 
 def split(value):
@@ -155,50 +145,27 @@
     left(acc, q_ref, p_ref)
 
 
-def first_kernel(count, sources, order, hidden_ref, *refs):
-    parts = refs[:count]
-    init_ref, acc_ref, turned = refs[count:]
-
-    @pl.when(pl.program_id(0) == 0)
-    def _():
-        turn(order, hidden_ref, turned, sources)
-
-    data = jnp.concatenate([p[...] for p in parts], axis=0)
-    acc_ref[...] = init_ref[...].astype(F32) + jnp.dot(
-        turned[...], data, preferred_element_type=F32
-    )
-
-
-def product(order, hidden, parts, init, q_turned=None, first=0, tile=256):
-    rows = init.shape[0]
+def product(order, hidden, parts, init, q_turned, tile=256):
+    rows, width = init.shape
     slots, feats = hidden.shape
     sources = order.shape[0]
-    width = parts[0].shape[1]
-    base = first // tile
-    in_specs = [pl.BlockSpec((slots, feats), lambda i, order: (0, 0))]
-    in_specs += [pl.BlockSpec((p.shape[0], tile), lambda i, order: (0, i)) for p in parts]
-    in_specs += [pl.BlockSpec((rows, tile), lambda i, order: (0, i + base))]
-    out_specs = [pl.BlockSpec((rows, tile), lambda i, order: (0, i))]
-    out_shape = [jax.ShapeDtypeStruct((rows, width), F32)]
-    args = (order, hidden, *parts, init)
-    kernel = first_kernel
-    if q_turned is not None:
-        kernel = product_kernel
-        thin = q_turned.shape[1]
-        in_specs += [pl.BlockSpec((tile, thin), lambda i, order: (i + base, 0))]
-        out_specs += [pl.BlockSpec((rows, thin // 2), lambda i, order: (0, 0))]
-        out_shape += [jax.ShapeDtypeStruct((rows, thin // 2), F32)]
-        args += (q_turned,)
-    return pl.pallas_call(
-        functools.partial(kernel, len(parts), sources),
+    thin = q_turned.shape[1]
+    flat = pl.BlockSpec((rows, tile), lambda i, order: (0, i))
+    return pl.pallas_call(
+        functools.partial(product_kernel, len(parts), sources),
         grid_spec=pltpu.PrefetchScalarGridSpec(
             num_scalar_prefetch=1,
             grid=(width // tile,),
-            in_specs=in_specs,
-            out_specs=out_specs,
+            in_specs=[pl.BlockSpec((slots, feats), lambda i, order: (0, 0))]
+            + [pl.BlockSpec((p.shape[0], tile), lambda i, order: (0, i)) for p in parts]
+            + [flat, pl.BlockSpec((tile, thin), lambda i, order: (i, 0))],
+            out_specs=[flat, pl.BlockSpec((rows, thin // 2), lambda i, order: (0, 0))],
             scratch_shapes=[pltpu.VMEM((feats, sources * CAP), BF16)],
         ),
-        out_shape=out_shape,
+        out_shape=[
+            jax.ShapeDtypeStruct((rows, width), F32),
+            jax.ShapeDtypeStruct((rows, thin // 2), F32),
+        ],
         cost_estimate=pl.CostEstimate(
             flops=2 * feats * sources * CAP * width,
             bytes_accessed=rows * width * 8 + sources * CAP * (feats + width) * 2,
@@ -206,7 +173,7 @@
         ),
         compiler_params=pltpu.CompilerParams(vmem_limit_bytes=40 << 20),
         name="product",
-    )(*args)
+    )(order, hidden, *parts, init, q_turned)
 
 
 def left_kernel(count, sources, order, hidden_hbm, *refs):
@@ -234,10 +201,10 @@
         (((0,), (0,)), ((), ())),
         preferred_element_type=F32,
     )
-    out_ref[...] = p_ref[...].T + (more[:rank] + more[rank:])
-
-
-def left_last(order, hidden, parts, q_turned, p_rest):
+    out_ref[...] = p_ref[...] + (more[:rank] + more[rank:])
+
+
+def left_share(order, hidden, parts, q_turned, p_rest):
     vmem = pl.BlockSpec(memory_space=pltpu.VMEM)
     sources = order.shape[0]
     feats = hidden.shape[1]
@@ -246,42 +213,57 @@
         in_specs=[pl.BlockSpec(memory_space=pltpu.SMEM), pl.BlockSpec(memory_space=pl.ANY)]
         + [vmem] * (len(parts) + 2),
         out_specs=vmem,
-        out_shape=jax.ShapeDtypeStruct(p_rest.shape[::-1], F32),
+        out_shape=jax.ShapeDtypeStruct(p_rest.shape, F32),
         scratch_shapes=[
             pltpu.VMEM((sources * CAP, feats), BF16),
             pltpu.SemaphoreType.DMA((sources,)),
         ],
         compiler_params=pltpu.CompilerParams(vmem_limit_bytes=16 << 20),
-        name="left_last",
+        name="left_share",
     )(order, hidden, *parts, q_turned, p_rest)
 
 
-def tail_kernel(sources, order, hidden_ref, *refs):
-    part_ref, acc_ref, high_ref, low_ref, turned = refs
-
-    @pl.when(pl.program_id(0) == 0)
-    def _():
-        turn(order, hidden_ref, turned, sources)
-
-    acc = acc_ref[...] + jnp.dot(turned[...], part_ref[...], preferred_element_type=F32)
-    high_ref[...], low_ref[...] = split(acc)
-
-
-def tail(order, hidden, part, acc, tile=256):
+def tail_kernel(count, sources, tile, order, hidden_hbm, *refs):
+    parts = refs[:count]
+    acc_ref, high_ref, low_ref, held, turned, sem = refs[count:]
+    copies = [
+        pltpu.make_async_copy(
+            hidden_hbm.at[pl.ds(pl.multiple_of(order[j] * CAP, CAP), CAP)],
+            held.at[pl.ds(j * CAP, CAP)],
+            sem.at[j],
+        )
+        for j in range(sources)
+    ]
+    for copy in copies:
+        copy.start()
+    for copy in copies:
+        copy.wait()
+    for j in range(0, sources * CAP, 2 * CAP):
+        turned[:, j : j + 2 * CAP] = held[j : j + 2 * CAP, :].T
+
+    @pl.loop(0, acc_ref.shape[1] // tile)
+    def _(i):
+        cols = pl.ds(pl.multiple_of(i * tile, tile), tile)
+        data = jnp.concatenate([p[:, cols] for p in parts], axis=0)
+        acc = acc_ref[:, cols] + jnp.dot(turned[...], data, preferred_element_type=F32)
+        high_ref[:, cols], low_ref[:, cols] = split(acc)
+
+
+def tail(order, hidden, parts, acc, tile=256):
     rows, width = acc.shape
-    slots, feats = hidden.shape
+    feats = hidden.shape[1]
     sources = order.shape[0]
-    flat = pl.BlockSpec((rows, tile), lambda i, order: (0, i))
-    return pl.pallas_call(
-        functools.partial(tail_kernel, sources),
-        grid_spec=pltpu.PrefetchScalarGridSpec(
-            num_scalar_prefetch=1,
-            grid=(width // tile,),
-            in_specs=[pl.BlockSpec((slots, feats), lambda i, order: (0, 0))]
-            + [pl.BlockSpec((part.shape[0], tile), lambda i, order: (0, i)), flat],
-            out_specs=[flat, flat],
-            scratch_shapes=[pltpu.VMEM((feats, sources * CAP), BF16)],
-        ),
+    vmem = pl.BlockSpec(memory_space=pltpu.VMEM)
+    return pl.pallas_call(
+        functools.partial(tail_kernel, len(parts), sources, tile),
+        in_specs=[pl.BlockSpec(memory_space=pltpu.SMEM), pl.BlockSpec(memory_space=pl.ANY)]
+        + [vmem] * (len(parts) + 1),
+        out_specs=[vmem, vmem],
+        scratch_shapes=[
+            pltpu.VMEM((sources * CAP, feats), BF16),
+            pltpu.VMEM((feats, sources * CAP), BF16),
+            pltpu.SemaphoreType.DMA((sources,)),
+        ],
         out_shape=[jax.ShapeDtypeStruct((rows, width), BF16)] * 2,
         cost_estimate=pl.CostEstimate(
             flops=2 * feats * sources * CAP * width,
@@ -290,16 +272,10 @@
         ),
         compiler_params=pltpu.CompilerParams(vmem_limit_bytes=32 << 20),
         name="tail",
-    )(order, hidden, part, acc)
-
-
-def factors_kernel(a_ref, b_ref, c_ref, d_ref, high_hbm, low_hbm, p_ref, q_ref, high, low, sems):
-    copies = [
-        pltpu.make_async_copy(high_hbm, high, sems.at[0]),
-        pltpu.make_async_copy(low_hbm, low, sems.at[1]),
-    ]
-    for copy in copies:
-        copy.start()
+    )(order, hidden, *parts, acc)
+
+
+def factors_kernel(a_ref, b_ref, c_ref, d_ref, high_ref, low_ref, p_ref, q_ref, turned_ref):
     current = (a_ref[...] + b_ref[...]) + (c_ref[...] + d_ref[...])
     count = current.shape[0]
     row = lax.broadcasted_iota(jnp.int32, (count, 1), 0)
@@ -311,77 +287,74 @@
         scale = jnp.where(row == i, lax.rsqrt(norm2), 1.0)
         current = current * scale - coeffs * vector
     p_ref[...] = current
-    p_high = current.astype(BF16)
-    p_low = (current - p_high.astype(F32)).astype(BF16)
+    p_high, p_low = split(current)
     p_both = jnp.concatenate([p_high, p_low], axis=0)
-    for copy in copies:
-        copy.wait()
+    turned_ref[...] = jnp.concatenate([p_high, p_both], axis=0).T
     for c in range(0, q_ref.shape[1], 512):
-        both = jnp.dot(p_both, high[:, c : c + 512], preferred_element_type=F32)
-        rest = jnp.dot(p_high, low[:, c : c + 512], preferred_element_type=F32)
+        both = jnp.dot(p_both, high_ref[:, c : c + 512], preferred_element_type=F32)
+        rest = jnp.dot(p_high, low_ref[:, c : c + 512], preferred_element_type=F32)
         q_ref[:, c : c + 512] = both[:count] + (both[count:] + rest)
 
 
 def factors(parts, high, low):
     rank = parts[0].shape[0]
     rows, width = high.shape
-    vmem, far = pl.BlockSpec(memory_space=pltpu.VMEM), pl.BlockSpec(memory_space=pl.ANY)
+    vmem = pl.BlockSpec(memory_space=pltpu.VMEM)
     return pl.pallas_call(
         factors_kernel,
-        in_specs=[vmem] * 4 + [far] * 2,
-        out_specs=[vmem] * 2,
+        in_specs=[vmem] * 6,
+        out_specs=[vmem] * 3,
         out_shape=[
             jax.ShapeDtypeStruct((rank, rows), F32),
             jax.ShapeDtypeStruct((rank, width), F32),
-        ],
-        scratch_shapes=[
-            pltpu.VMEM((rows, width), BF16),
-            pltpu.VMEM((rows, width), BF16),
-            pltpu.SemaphoreType.DMA((2,)),
+            jax.ShapeDtypeStruct((rows, 3 * rank), BF16),
         ],
         compiler_params=pltpu.CompilerParams(vmem_limit_bytes=24 << 20),
         name="factors",
     )(*parts, high, low)
 
 
-def finish_kernel(p_ref, a_ref, b_ref, c_ref, d_ref, high_ref, low_ref, out_ref, q_ref):
+def finish_kernel(tile, p_ref, a_ref, b_ref, c_ref, d_ref, high_ref, low_ref, out_hbm, q_ref, held, sems):
     q = (a_ref[...].astype(F32) + b_ref[...].astype(F32)) + (
         c_ref[...].astype(F32) + d_ref[...].astype(F32)
     )
     q = q * 0.125
     q_ref[...] = q
-    q_high = q.astype(BF16)
-    q_low = (q - q_high.astype(F32)).astype(BF16)
-    p = p_ref[...]
-    p_high = p.astype(BF16)
-    p_low = (p - p_high.astype(F32)).astype(BF16)
-    approx = lax.dot_general(
-        jnp.concatenate([p_high, p_high, p_low], axis=0),
-        jnp.concatenate([q_high, q_low, q_high], axis=0),
-        (((0,), (0,)), ((), ())),
-        preferred_element_type=F32,
-    )
-    acc = high_ref[...].astype(F32) + low_ref[...].astype(F32)
-    out_ref[...] = (acc - approx).astype(BF16)
-
-
-def finish(p_hat, parts, high, low, tile=256):
-    rank, rows = p_hat.shape
-    width = high.shape[1]
-    flat = pl.BlockSpec((rows, tile), lambda i: (0, i))
-    thin = pl.BlockSpec((rank, tile), lambda i: (0, i))
-    return pl.pallas_call(
-        finish_kernel,
-        grid=(width // tile,),
-        in_specs=[pl.BlockSpec((rank, rows), lambda i: (0, 0))] + [thin] * 4 + [flat] * 2,
-        out_specs=[flat, thin],
+    q_high, q_low = split(q)
+    stack = jnp.concatenate([q_high, q_low, q_high], axis=0)
+    copies = []
+    for c in range(0, high_ref.shape[1], tile):
+        approx = jnp.dot(p_ref[...], stack[:, c : c + tile], preferred_element_type=F32)
+        acc = high_ref[:, c : c + tile].astype(F32) + low_ref[:, c : c + tile].astype(F32)
+        held[:, c : c + tile] = (acc - approx).astype(BF16)
+        copy = pltpu.make_async_copy(
+            held.at[:, pl.ds(c, tile)], out_hbm.at[:, pl.ds(c, tile)], sems.at[c // tile]
+        )
+        copy.start()
+        copies.append(copy)
+    for copy in copies:
+        copy.wait()
+
+
+def finish(p_turned, parts, high, low, tile=256):
+    rows, width = high.shape
+    rank = parts[0].shape[0]
+    vmem = pl.BlockSpec(memory_space=pltpu.VMEM)
+    return pl.pallas_call(
+        functools.partial(finish_kernel, tile),
+        in_specs=[vmem] * 7,
+        out_specs=[pl.BlockSpec(memory_space=pl.ANY), vmem],
         out_shape=[
             jax.ShapeDtypeStruct((rows, width), BF16),
             jax.ShapeDtypeStruct((rank, width), F32),
         ],
-        compiler_params=pltpu.CompilerParams(vmem_limit_bytes=16 << 20),
+        scratch_shapes=[
+            pltpu.VMEM((rows, width), BF16),
+            pltpu.SemaphoreType.DMA((width // tile,)),
+        ],
+        compiler_params=pltpu.CompilerParams(vmem_limit_bytes=24 << 20),
         name="finish",
-    )(p_hat, *parts, high, low)
+    )(p_turned, *parts, high, low)
 
 
 def partner(value, k):
@@ -392,7 +365,7 @@
     me = lax.axis_index("exp").astype(jnp.int32)
     x, z = me // NZ, me % NZ
     ids = jnp.arange(NX, dtype=jnp.int32) * NZ + z
-    own, sent = pack(grad_out[0], routes[0].T, gates[0].T, ids)
+    own = pack(grad_out[0], routes[0].T, gates[0].T)
 
     b = {0: own}
     parts, order = [], []
@@ -415,21 +388,21 @@
     b[3] = move(b[2], 0, 1)
     b[5] = move(b[6], 0, -1)
     b[4] = move(b[3], 0, 1)
-    spread(GROUPS[0], sent)
+    spread(GROUPS[0], select([own], ids))
     for group in GROUPS[1:4]:
         spread(group, select([b[k] for k in group], ids))
     held = hidden[0, 0]
     q_turned = jnp.concatenate(split(q_init[0]), axis=0).T
-    (acc,) = product(jnp.concatenate(order[:3]), held, parts[:3], error[0, 0])
-    spread(GROUPS[4], select([b[k] for k in GROUPS[4]], ids, (acc,)))
-    acc, p_rest = product(order[3], held, parts[3:4], acc, q_turned)
-    p_local = left_last(order[-1], held, parts[-1:], q_turned, p_rest)
+    acc, p_rest = product(jnp.concatenate(order[:3]), held, parts[:3], error[0, 0], q_turned)
+    spread(GROUPS[4], select([b[k] for k in GROUPS[4]], ids, (p_rest,)))
+    p_rest = left_share(order[3], held, parts[3:4], q_turned, p_rest.T)
+    p_local = left_share(order[4], held, parts[4:], q_turned, p_rest)
     p_chip = p_local + partner(p_local, 1)
     p_parts = [p_chip] + [partner(p_chip, k) for k in (2, 4, 6)]
-    high, low = tail(order[-1], held, parts[-1], acc)
-    p_hat, q_local = factors(p_parts, high, low)
+    high, low = tail(jnp.concatenate(order[3:]), held, parts[3:], acc)
+    p_hat, q_local, p_turned = factors(p_parts, high, low)
     q_chip = (q_local + partner(q_local, 1)).astype(BF16)
-    new_error, q_mean = finish(p_hat, [q_chip] + [partner(q_chip, k) for k in (2, 4, 6)], high, low)
+    new_error, q_mean = finish(p_turned, [q_chip] + [partner(q_chip, k) for k in (2, 4, 6)], high, low)
     return new_error[None, None], p_hat[None], q_mean[None]
 
 

time: 186 us -> 179 us (0.962)
  local copies, waits for them, and re-layouts: 27 us -> 16 us
    unnamed x53 -> x47, local copies, waits for them, and re-layouts: 27 us -> 15.2 us
    pallas_call x4 -> x5, Pallas kernels: 6.12 us -> 11.1 us  [select(): pl.pallas_call(functools.partial(select_kernel, counts, experts), in_spec...]
    pallas_call x7, Pallas kernels: 42.4 us -> 37.6 us  [the longest x1 14.1 us: product(): pl.pallas_call(functools.partial(product_kernel, len(parts), sources), gr...]
    all_to_all x5, waiting for transfers between devices: 16 us -> 19.7 us  [spread(): lax.all_to_all(sent, 'exp', split_axis=0, concat_axis=0, tiled=True, axis...]
  transfers between devices with their start and end apart: 20 -> 20, of which waited for: 11 -> 12; matrix products, arithmetic and copies ran while one was open for 2% -> 2% of each run, Pallas kernels for 18% -> 20%
where the time goes in v2:
time: 179 us; the launch traced here: 178 us
  waiting for transfers between devices  61.1 us (34%)
  starting transfers between devices  49.1 us (27%)
  Pallas kernels  48.7 us (27%)
  local copies, waits for them, and re-layouts  16 us (9%)
  other arithmetic  2.02 us (1%)
    ppermute x7, waiting for transfers between devices, move(): return lax.ppermute(block, 'exp', pairs)  30.8 us
    all_to_all x5, starting transfers between devices, spread(): lax.all_to_all(sent, 'exp', split_axis=0, concat_axis=0, tiled=True, axis...  22.4 us
    all_to_all x5, waiting for transfers between devices, spread(): lax.all_to_all(sent, 'exp', split_axis=0, concat_axis=0, tiled=True, axis...  19.7 us
    ppermute x8, starting transfers between devices, partner(): return lax.ppermute(value, 'rep', [(i, i ^ k) for i in range(8)])  15.5 us
    unnamed x47, local copies, waits for them, and re-layouts  15.2 us
    pallas_call x1, Pallas kernels, product(): pl.pallas_call(functools.partial(product_kernel, len(parts), sources), gr...  14.1 us
    ppermute x7, starting transfers between devices, move(): return lax.ppermute(block, 'exp', pairs)  11.2 us
    pallas_call x5, Pallas kernels, select(): pl.pallas_call(functools.partial(select_kernel, counts, experts), in_spec...  11.1 us
  transfers between devices with their start and end apart: 20, of which 12 were waited for; matrix products, arithmetic and copies ran while one was open for 2% of the time, Pallas kernels for 20%

profile of v2, /device:TPU:1, one launch (start us, length us, event | category | flops | bytes accessed | tf_op | source)
XLA Modules:
  0.0 178.0 jit_solution(12288118851449359692)
XLA Ops:
  0.7 1.9 %pack.1.refs_0_ = bf16[136,2048]{1,0:T(8,128)(2,1)} custom-call(bf16[128,2048]{1,0:T(8,128)(2,1)} %bitcast.41, s32[8,128]{1,0:T(8,128)} %bitcast.42, f32[8,128]{1,0:T(8,128)} %bitcast.43), custom_call_target="tpu_custom_call" | custom-call | bytes 1048576 | tf_op jit(solution)/shard_map/pack/pallas_call | solution.py:103
  2.6 1.1 copy-done.7
  3.6 2.1 %select.17 = bf16[256,2048]{1,0:T(8,128)(2,1)} custom-call(s32[4]{0:T(128)S(1)} %fusion.7.ids_ref, bf16[136,2048]{1,0:T(8,128)(2,1)S(1)} %copy-done.7), custom_call_target="tpu_custom_call" | custom-call | flops 134217728 | bytes 1605632 | tf_op jit(solution)/shard_map/select/pallas_call | solution.py:73
  5.7 4.8 %all-to-all-start = ((bf16[4,64,2048]{2,1,0:T(8,128)(2,1)}), bf16[4,64,2048]{2,1,0:T(8,128)(2,1)S(1)}, u32[]{:S(2)}, u32[]{:S(2)}) async-start(bf16[4,64,2048]{2,1,0:T(8,128)(2,1)} %bitcast.6), calls=%async_computation | async-start | bytes 2097152 | tf_op jit(solution)/shard_map/all_to_all | solution.py:376
  10.6 1.6 collective-permute-start
  12.2 4.0 %collective-permute-start.4 = (bf16[136,2048]{1,0:T(8,128)(2,1)S(1)}, bf16[136,2048]{1,0:T(8,128)(2,1)S(1)}, u32[]{:S(2)}, u32[]{:S(2)}) collective-permute-start(bf16[136,2048]{1,0:T(8,128)(2,1)S(1)} %copy-done.8), channel_id=1, source_target_pairs={{0,7},{1,0},{2,1},{3,2},{4,3},{5,4},{6,5},{7,6},{8,15},{9,8},{10,9... | collective-permute-start | bytes 1671176 | tf_op jit(solution)/shard_map/ppermute | solution.py:26
  16.2 11.9 %collective-permute-done.refs_0_ = bf16[136,2048]{1,0:T(8,128)(2,1)S(1)} collective-permute-done((bf16[136,2048]{1,0:T(8,128)(2,1)S(1)}, bf16[136,2048]{1,0:T(8,128)(2,1)S(1)}, u32[]{:S(2)}, u32[]{:S(2)}) %collective-permute-start) | collective-permute-done | bytes 557088 | tf_op jit(solution)/shard_map/ppermute | solution.py:26
  28.2 2.8 %select.18 = bf16[512,2048]{1,0:T(8,128)(2,1)} custom-call(s32[4]{0:T(128)S(1)} %fusion.7.ids_ref, bf16[136,2048]{1,0:T(8,128)(2,1)S(1)} %collective-permute-done.refs_0_, bf16[136,2048]{1,0:T(8,128)(2,1)S(1)} %collective-permute-done.4.refs_1_), custom_call_target="tpu_custom_call" | custom-call | flops 268435456 | bytes 3211264 | tf_op jit(solution)/shard_map/select/pallas_call | solution.py:73
  31.8 1.0 copy-done.11
  32.8 3.9 %all-to-all-start.1 = ((bf16[4,128,2048]{2,1,0:T(8,128)(2,1)}), bf16[4,128,2048]{2,1,0:T(8,128)(2,1)S(1)}, u32[]{:S(2)}, u32[]{:S(2)}) async-start(bf16[4,128,2048]{2,1,0:T(8,128)(2,1)} %bitcast.8), calls=%async_computation.1 | async-start | bytes 4194304 | tf_op jit(solution)/shard_map/all_to_all | solution.py:376
  36.7 2.7 %collective-permute-start.5 = (bf16[136,2048]{1,0:T(8,128)(2,1)}, bf16[136,2048]{1,0:T(8,128)(2,1)S(1)}, u32[]{:S(2)}, u32[]{:S(2)}) collective-permute-start(bf16[136,2048]{1,0:T(8,128)(2,1)} %copy-done.15), channel_id=1, source_target_pairs={{0,7},{1,0},{2,1},{3,2},{4,3},{5,4},{6,5},{7,6},{8,15},{9,8},{10,9... | collective-permute-start | bytes 1671176 | tf_op jit(solution)/shard_map/ppermute | solution.py:26
  39.4 10.5 %collective-permute-done.1.refs_0_ = bf16[136,2048]{1,0:T(8,128)(2,1)S(1)} collective-permute-done((bf16[136,2048]{1,0:T(8,128)(2,1)S(1)}, bf16[136,2048]{1,0:T(8,128)(2,1)S(1)}, u32[]{:S(2)}, u32[]{:S(2)}) %collective-permute-start.1) | collective-permute-done | bytes 557088 | tf_op jit(solution)/shard_map/ppermute | solution.py:26
  49.9 2.8 %select.19 = bf16[512,2048]{1,0:T(8,128)(2,1)} custom-call(s32[4]{0:T(128)S(1)} %fusion.7.ids_ref, bf16[136,2048]{1,0:T(8,128)(2,1)S(1)} %collective-permute-done.1.refs_0_, bf16[136,2048]{1,0:T(8,128)(2,1)S(1)} %collective-permute-done.5.refs_1_), custom_call_target="tpu_custom_call" | custom-call | flops 268435456 | bytes 3211264 | tf_op jit(solution)/shard_map/select/pallas_call | solution.py:73
  53.5 7.4 %all-to-all-done.1 = bf16[4,128,2048]{2,1,0:T(8,128)(2,1)S(1)} async-done(((bf16[4,128,2048]{2,1,0:T(8,128)(2,1)}), bf16[4,128,2048]{2,1,0:T(8,128)(2,1)S(1)}, u32[]{:S(2)}, u32[]{:S(2)}) %all-to-all-start.1) | async-done | bytes 2097184 | tf_op jit(solution)/shard_map/all_to_all | solution.py:376
  60.9 4.5 %all-to-all-start.2 = ((bf16[4,128,2048]{2,1,0:T(8,128)(2,1)}), bf16[4,128,2048]{2,1,0:T(8,128)(2,1)}, u32[]{:S(2)}, u32[]{:S(2)}) async-start(bf16[4,128,2048]{2,1,0:T(8,128)(2,1)} %bitcast.10), calls=%async_computation.2 | async-start | bytes 4194304 | tf_op jit(solution)/shard_map/all_to_all | solution.py:376
  65.5 2.7 %collective-permute-start.6 = (bf16[136,2048]{1,0:T(8,128)(2,1)}, bf16[136,2048]{1,0:T(8,128)(2,1)}, u32[]{:S(2)}, u32[]{:S(2)}) collective-permute-start(bf16[136,2048]{1,0:T(8,128)(2,1)} %copy-done.14), channel_id=1, source_target_pairs={{0,7},{1,0},{2,1},{3,2},{4,3},{5,4},{6,5},{7,6},{8,15},{9,8},{10,9... | collective-permute-start | bytes 1671176 | tf_op jit(solution)/shard_map/ppermute | solution.py:26
  68.1 1.3 copy.19
  69.5 8.3 %collective-permute-done.2.refs_0_ = bf16[136,2048]{1,0:T(8,128)(2,1)S(1)} collective-permute-done((bf16[136,2048]{1,0:T(8,128)(2,1)S(1)}, bf16[136,2048]{1,0:T(8,128)(2,1)S(1)}, u32[]{:S(2)}, u32[]{:S(2)}) %collective-permute-start.2) | collective-permute-done | bytes 557088 | tf_op jit(solution)/shard_map/ppermute | solution.py:26
  77.8 2.2 %select.21 = bf16[512,2048]{1,0:T(8,128)(2,1)S(1)} custom-call(s32[4]{0:T(128)S(1)} %fusion.7.ids_ref, bf16[136,2048]{1,0:T(8,128)(2,1)S(1)} %collective-permute-done.2.refs_0_, bf16[136,2048]{1,0:T(8,128)(2,1)} %collective-permute-done.6.refs_1_), custom_call_target="tpu_custom_call" | custom-call | flops 268435456 | bytes 3211264 | tf_op jit(solution)/shard_map/select/pallas_call | solution.py:73
  80.0 1.4 copy-done.1
  81.5 7.2 %all-to-all-done.2 = bf16[4,128,2048]{2,1,0:T(8,128)(2,1)} async-done(((bf16[4,128,2048]{2,1,0:T(8,128)(2,1)}), bf16[4,128,2048]{2,1,0:T(8,128)(2,1)}, u32[]{:S(2)}, u32[]{:S(2)}) %all-to-all-start.2) | async-done | bytes 2097184 | tf_op jit(solution)/shard_map/all_to_all | solution.py:376
  88.7 4.7 %all-to-all-start.4 = ((bf16[4,128,2048]{2,1,0:T(8,128)(2,1)}), bf16[4,128,2048]{2,1,0:T(8,128)(2,1)}, u32[]{:S(2)}, u32[]{:S(2)}) async-start(bf16[4,128,2048]{2,1,0:T(8,128)(2,1)} %bitcast.35), calls=%async_computation.4 | async-start | bytes 4194304 | tf_op jit(solution)/shard_map/all_to_all | solution.py:376
  93.6 1.5 fusion
  95.6 2.0 %copy-done.17 = bf16[1,1,768,2048]{3,2,1,0:T(8,128)(2,1)S(1)} copy-done((bf16[1,1,768,2048]{3,2,1,0:T(8,128)(2,1)S(1)}, bf16[1,1,768,2048]{3,2,1,0:T(8,128)(2,1)}, u32[]{:S(2)}) %copy-start.17) | copy-done | bytes 3145752
  97.6 14.1 %product.1 = (f32[768,2048]{1,0:T(8,128)}, f32[768,32]{1,0:T(8,128)S(1)}) custom-call(s32[20]{0:T(128)S(1)} %pad_add_fusion.order, bf16[2048,768]{1,0:T(8,128)(2,1)S(1)} %bitcast.31, bf16[256,2048]{1,0:T(8,128)(2,1)S(1)} %bitcast.38, bf16[512,2048]{1,0:T(8,128)(2,1)S(1)} %bitcast.37, bf16[512,2048]{1,0:T(8,128)(2,1)} %bitcast.11.refs_2_, ...), custom_call_target="tpu_custom_call" | custom-call | flops 4026531840 | bytes 19791872 | tf_op jit(solution)/shard_map/product/pallas_call | solution.py:154
  111.7 1.1 select.20
  112.8 1.0 copy-done.6
  113.8 2.1 %all-to-all-done.4 = bf16[4,128,2048]{2,1,0:T(8,128)(2,1)} async-done(((bf16[4,128,2048]{2,1,0:T(8,128)(2,1)}), bf16[4,128,2048]{2,1,0:T(8,128)(2,1)}, u32[]{:S(2)}, u32[]{:S(2)}) %all-to-all-start.4) | async-done | bytes 2097184 | tf_op jit(solution)/shard_map/all_to_all | solution.py:376
  115.9 4.4 %all-to-all-start.3 = ((bf16[4,64,2048]{2,1,0:T(8,128)(2,1)}), bf16[4,64,2048]{2,1,0:T(8,128)(2,1)}, u32[]{:S(2)}, u32[]{:S(2)}) async-start(bf16[4,64,2048]{2,1,0:T(8,128)(2,1)} %bitcast.36), calls=%async_computation.3 | async-start | bytes 2097152 | tf_op jit(solution)/shard_map/all_to_all | solution.py:376
  121.1 1.0 copy-done.4
  122.2 0.9 copy-done.16
  123.1 4.0 %left_share.2.refs_2_ = f32[32,768]{1,0:T(8,128)S(1)} custom-call(s32[8]{0:T(128)S(1)} %get-tuple-element.23.order, bf16[2048,768]{1,0:T(8,128)(2,1)S(1)} %bitcast.32, bf16[512,2048]{1,0:T(8,128)(2,1)} %bitcast.18.refs_0_, bf16[2048,64]{1,0:T(8,128)(2,1)S(1)} %copy-done.4, f32[32,768]{1,0:T(8,128)S(1)} %bitcast.39), custom_call_target="tpu_custom_call" | custom-call | tf_op jit(solution)/shard_map/left_share/pallas_call | solution.py:211
  127.1 3.0 %all-to-all-done.3 = bf16[4,64,2048]{2,1,0:T(8,128)(2,1)} async-done(((bf16[4,64,2048]{2,1,0:T(8,128)(2,1)}), bf16[4,64,2048]{2,1,0:T(8,128)(2,1)}, u32[]{:S(2)}, u32[]{:S(2)}) %all-to-all-start.3) | async-done | bytes 1048608 | tf_op jit(solution)/shard_map/all_to_all | solution.py:376
  130.1 1.0 copy-done.5
  131.1 2.6 %left_share.3 = f32[32,768]{1,0:T(8,128)S(1)} custom-call(s32[4]{0:T(128)S(1)} %fusion.9.order, bf16[2048,768]{1,0:T(8,128)(2,1)S(1)} %bitcast.33, bf16[256,2048]{1,0:T(8,128)(2,1)} %bitcast.16.refs_0_.refs_1_, bf16[2048,64]{1,0:T(8,128)(2,1)S(1)} %copy-done.5, f32[32,768]{1,0:T(8,128)S(1)} %left_share.2.refs_2_), custom_call_target="tpu_custom_call" | custom-call | tf_op jit(solution)/shard_map/left_share/pallas_call | solution.py:211
  133.7 6.2 %collective-permute-start.7 = (f32[32,768]{1,0:T(8,128)S(1)}, f32[32,768]{1,0:T(8,128)S(1)}, u32[]{:S(2)}, u32[]{:S(2)}) collective-permute-start(f32[32,768]{1,0:T(8,128)S(1)} %left_share.3), channel_id=1, source_target_pairs={{0,32},{32,0},{64,96},{96,64},{128,160},{160,128},{192,224},{224,1... | collective-permute-start | bytes 294920 | tf_op jit(solution)/shard_map/ppermute | solution.py:361
  140.1 0.9 collective-permute-done.7
  140.9 1.4 collective-permute-start.8
  142.4 2.7 %collective-permute-start.9 = (f32[32,768]{1,0:T(8,128)S(1)}, f32[32,768]{1,0:T(8,128)S(1)}, u32[]{:S(2)}, u32[]{:S(2)}) collective-permute-start(f32[32,768]{1,0:T(8,128)S(1)} %add.65.a_ref), channel_id=1, source_target_pairs={{0,128},{32,160},{64,192},{96,224},{128,0},{160,32},{192,64},{224,... | collective-permute-start | bytes 294920 | tf_op jit(solution)/shard_map/ppermute | solution.py:361
  145.1 2.8 %copy-done.2 = f32[768,2048]{1,0:T(8,128)S(1)} copy-done((f32[768,2048]{1,0:T(8,128)S(1)}, f32[768,2048]{1,0:T(8,128)}, u32[]{:S(2)}) %copy-start.2) | copy-done | bytes 6291480
  147.8 7.9 %tail.1 = (bf16[768,2048]{1,0:T(8,128)(2,1)S(1)}, bf16[768,2048]{1,0:T(8,128)(2,1)S(1)}) custom-call(s32[12]{0:T(128)S(1)} %pad_add_fusion.1.order, bf16[2048,768]{1,0:T(8,128)(2,1)S(1)} %bitcast.34, bf16[512,2048]{1,0:T(8,128)(2,1)} %bitcast.18.refs_0_, bf16[256,2048]{1,0:T(8,128)(2,1)} %bitcast.16.refs_0_.refs_1_, f32[768,2048]{1,0:T(8,128)S(1)} %copy-done.2), custom_call_target="tpu_custom_call" | custom-call | flops 2415919104 | bytes 16908288 | tf_op jit(solution)/shard_map/tail/pallas_call | solution.py:257
  155.8 4.2 %factors.1 = (f32[32,768]{1,0:T(8,128)}, f32[32,2048]{1,0:T(8,128)S(1)}, bf16[768,96]{1,0:T(8,128)(2,1)S(1)}) custom-call(f32[32,768]{1,0:T(8,128)S(1)} %add.65.a_ref, f32[32,768]{1,0:T(8,128)S(1)} %collective-permute-done.8.b_ref, f32[32,768]{1,0:T(8,128)S(1)} %collective-permute-done.9.c_ref, f32[32,768]{1,0:T(8,128)S(1)} %collective-permute-done.10.d_ref, ...), custom_call_target="tpu_custom_call" | custom-call | tf_op jit(solution)/shard_map/factors/pallas_call | solution.py:303
  159.9 1.1 collective-permute-start.11
  161.0 1.2 collective-permute-done.11
  162.4 3.9 %collective-permute-start.13 = (bf16[32,2048]{1,0:T(8,128)(2,1)S(1)}, bf16[32,2048]{1,0:T(8,128)(2,1)S(1)}, u32[]{:S(2)}, u32[]{:S(2)}) collective-permute-start(bf16[32,2048]{1,0:T(8,128)(2,1)S(1)} %add_convert_fusion.a_ref), channel_id=1, source_target_pairs={{0,128},{32,160},{64,192},{96,224},{128,0},{160,32},{192,64},{224,... | collective-permute-start | bytes 393224 | tf_op jit(solution)/shard_map/ppermute | solution.py:361
  167.0 5.4 %collective-permute-done.13.c_ref = bf16[32,2048]{1,0:T(8,128)(2,1)S(1)} collective-permute-done((bf16[32,2048]{1,0:T(8,128)(2,1)S(1)}, bf16[32,2048]{1,0:T(8,128)(2,1)S(1)}, u32[]{:S(2)}, u32[]{:S(2)}) %collective-permute-start.13) | collective-permute-done | bytes 131104 | tf_op jit(solution)/shard_map/ppermute | solution.py:361
  172.4 2.5 %collective-permute-done.14.d_ref = bf16[32,2048]{1,0:T(8,128)(2,1)S(1)} collective-permute-done((bf16[32,2048]{1,0:T(8,128)(2,1)S(1)}, bf16[32,2048]{1,0:T(8,128)(2,1)S(1)}, u32[]{:S(2)}, u32[]{:S(2)}) %collective-permute-start.14) | collective-permute-done | bytes 131104 | tf_op jit(solution)/shard_map/ppermute | solution.py:361
  174.9 2.9 %finish.1 = (bf16[768,2048]{1,0:T(8,128)(2,1)}, f32[32,2048]{1,0:T(8,128)}) custom-call(bf16[768,96]{1,0:T(8,128)(2,1)S(1)} %get-tuple-element.16.p_ref, bf16[32,2048]{1,0:T(8,128)(2,1)S(1)} %add_convert_fusion.a_ref, bf16[32,2048]{1,0:T(8,128)(2,1)S(1)} %collective-permute-done.12.b_ref, bf16[32,2048]{1,0:T(8,128)(2,1)S(1)} %collective-permute-done.13.c_ref, ...), custom_call_target="tpu_custom_call" | custom-call | tf_op jit(solution)/shard_map/finish/pallas_call | solution.py:343
  (62 shorter events, 4.1 us)
Async XLA Ops:
  2.6 1.1 copy-start.7
  3.6 6.9 %copy-start.8 = (bf16[136,2048]{1,0:T(8,128)(2,1)S(1)}, bf16[136,2048]{1,0:T(8,128)(2,1)}, u32[]{:S(2)}) copy-start(bf16[136,2048]{1,0:T(8,128)(2,1)} %pack.1.refs_0_) | copy-start | bytes 1671172
  5.7 26.1 %all-to-all-start = ((bf16[4,64,2048]{2,1,0:T(8,128)(2,1)}), bf16[4,64,2048]{2,1,0:T(8,128)(2,1)S(1)}, u32[]{:S(2)}, u32[]{:S(2)}) async-start(bf16[4,64,2048]{2,1,0:T(8,128)(2,1)} %bitcast.6), calls=%async_computation | async-start | bytes 2097152 | tf_op jit(solution)/shard_map/all_to_all | solution.py:376
  10.6 17.6 %collective-permute-start = (bf16[136,2048]{1,0:T(8,128)(2,1)S(1)}, bf16[136,2048]{1,0:T(8,128)(2,1)S(1)}, u32[]{:S(2)}, u32[]{:S(2)}) collective-permute-start(bf16[136,2048]{1,0:T(8,128)(2,1)S(1)} %copy-done.8), channel_id=1, source_target_pairs={{0,1},{1,2},{2,3},{3,4},{4,5},{5,6},{6,7},{7,0},{8,9},{9,10},{10,1... | collective-permute-start | bytes 1671176 | tf_op jit(solution)/shard_map/ppermute | solution.py:26
  12.2 16.0 %collective-permute-start.4 = (bf16[136,2048]{1,0:T(8,128)(2,1)S(1)}, bf16[136,2048]{1,0:T(8,128)(2,1)S(1)}, u32[]{:S(2)}, u32[]{:S(2)}) collective-permute-start(bf16[136,2048]{1,0:T(8,128)(2,1)S(1)} %copy-done.8), channel_id=1, source_target_pairs={{0,7},{1,0},{2,1},{3,2},{4,3},{5,4},{6,5},{7,6},{8,15},{9,8},{10,9... | collective-permute-start | bytes 1671176 | tf_op jit(solution)/shard_map/ppermute | solution.py:26
  31.0 0.8 copy-start.15
  31.8 1.0 copy-start.11
  32.8 28.1 %all-to-all-start.1 = ((bf16[4,128,2048]{2,1,0:T(8,128)(2,1)}), bf16[4,128,2048]{2,1,0:T(8,128)(2,1)S(1)}, u32[]{:S(2)}, u32[]{:S(2)}) async-start(bf16[4,128,2048]{2,1,0:T(8,128)(2,1)} %bitcast.8), calls=%async_computation.1 | async-start | bytes 4194304 | tf_op jit(solution)/shard_map/all_to_all | solution.py:376
  36.7 31.4 %copy-start.18 = (f32[1,32,2048]{2,1,0:T(8,128)S(1)}, f32[1,32,2048]{2,1,0:T(8,128)}, u32[]{:S(2)}) copy-start(f32[1,32,2048]{2,1,0:T(8,128)} %param.21) | copy-start | bytes 786436
  36.7 13.2 %collective-permute-start.1 = (bf16[136,2048]{1,0:T(8,128)(2,1)S(1)}, bf16[136,2048]{1,0:T(8,128)(2,1)S(1)}, u32[]{:S(2)}, u32[]{:S(2)}) collective-permute-start(bf16[136,2048]{1,0:T(8,128)(2,1)S(1)} %collective-permute-done.refs_0_), channel_id=1, source_target_pairs={{0,1},{1,2},{2,3},{3,4},{4,5},{5,6},{6,7},{7,0},{8,9},{9,10},{10,1... | collective-permute-start | bytes 1671176 | tf_op jit(solution)/shard_map/ppermute | solution.py:26
  36.7 13.2 %collective-permute-start.5 = (bf16[136,2048]{1,0:T(8,128)(2,1)}, bf16[136,2048]{1,0:T(8,128)(2,1)S(1)}, u32[]{:S(2)}, u32[]{:S(2)}) collective-permute-start(bf16[136,2048]{1,0:T(8,128)(2,1)} %copy-done.15), channel_id=1, source_target_pairs={{0,7},{1,0},{2,1},{3,2},{4,3},{5,4},{6,5},{7,6},{8,15},{9,8},{10,9... | collective-permute-start | bytes 1671176 | tf_op jit(solution)/shard_map/ppermute | solution.py:26
  52.7 0.8 copy-start.14
  60.9 19.1 %copy-start.9 = (bf16[4,128,2048]{2,1,0:T(8,128)(2,1)}, bf16[4,128,2048]{2,1,0:T(8,128)(2,1)S(1)}, u32[]{:S(2)}) copy-start(bf16[4,128,2048]{2,1,0:T(8,128)(2,1)S(1)} %all-to-all-done.1) | copy-start | bytes 6291460
  60.9 27.8 %all-to-all-start.2 = ((bf16[4,128,2048]{2,1,0:T(8,128)(2,1)}), bf16[4,128,2048]{2,1,0:T(8,128)(2,1)}, u32[]{:S(2)}, u32[]{:S(2)}) async-start(bf16[4,128,2048]{2,1,0:T(8,128)(2,1)} %bitcast.10), calls=%async_computation.2 | async-start | bytes 4194304 | tf_op jit(solution)/shard_map/all_to_all | solution.py:376
  65.4 12.4 %collective-permute-start.2 = (bf16[136,2048]{1,0:T(8,128)(2,1)S(1)}, bf16[136,2048]{1,0:T(8,128)(2,1)S(1)}, u32[]{:S(2)}, u32[]{:S(2)}) collective-permute-start(bf16[136,2048]{1,0:T(8,128)(2,1)S(1)} %collective-permute-done.1.refs_0_), channel_id=1, source_target_pairs={{0,1},{1,2},{2,3},{3,4},{4,5},{5,6},{6,7},{7,0},{8,9},{9,10},{10,1... | collective-permute-start | bytes 1671176 | tf_op jit(solution)/shard_map/ppermute | solution.py:26
  65.5 12.3 %collective-permute-start.6 = (bf16[136,2048]{1,0:T(8,128)(2,1)}, bf16[136,2048]{1,0:T(8,128)(2,1)}, u32[]{:S(2)}, u32[]{:S(2)}) collective-permute-start(bf16[136,2048]{1,0:T(8,128)(2,1)} %copy-done.14), channel_id=1, source_target_pairs={{0,7},{1,0},{2,1},{3,2},{4,3},{5,4},{6,5},{7,6},{8,15},{9,8},{10,9... | collective-permute-start | bytes 1671176 | tf_op jit(solution)/shard_map/ppermute | solution.py:26
  69.4 24.0 %copy-start.19 = (s32[8]{0:T(128)S(1)}, s32[8]{0:T(128)}, u32[]{:S(2)}) copy-start(s32[8]{0:T(128)} %constant.77) | copy-start | bytes 100
  69.4 24.0 %copy-start.20 = (s32[8]{0:T(128)S(1)}, s32[8]{0:T(128)}, u32[]{:S(2)}) copy-start(s32[8]{0:T(128)} %constant.80) | copy-start | bytes 100
  69.4 24.1 %copy-start.21 = (s32[8]{0:T(128)S(1)}, s32[8]{0:T(128)}, u32[]{:S(2)}) copy-start(s32[8]{0:T(128)} %constant.79) | copy-start | bytes 100
  69.5 24.1 %copy-start.22 = (s32[8]{0:T(128)S(1)}, s32[8]{0:T(128)}, u32[]{:S(2)}) copy-start(s32[8]{0:T(128)} %constant.78) | copy-start | bytes 100
  77.8 10.9 %copy-start.13 = (bf16[136,2048]{1,0:T(8,128)(2,1)}, bf16[136,2048]{1,0:T(8,128)(2,1)S(1)}, u32[]{:S(2)}) copy-start(bf16[136,2048]{1,0:T(8,128)(2,1)S(1)} %collective-permute-done.2.refs_0_) | copy-start | bytes 1671172
  80.0 1.4 copy-start.1
  88.7 6.8 %copy-start = (bf16[1,1,2048,768]{3,2,1,0:T(8,128)(2,1)S(1)}, bf16[1,1,2048,768]{3,2,1,0:T(8,128)(2,1)}, u32[]{:S(2)}) copy-start(bf16[1,1,2048,768]{3,2,1,0:T(8,128)(2,1)} %param.19) | copy-start | bytes 9437188
  88.7 27.2 %all-to-all-start.4 = ((bf16[4,128,2048]{2,1,0:T(8,128)(2,1)}), bf16[4,128,2048]{2,1,0:T(8,128)(2,1)}, u32[]{:S(2)}, u32[]{:S(2)}) async-start(bf16[4,128,2048]{2,1,0:T(8,128)(2,1)} %bitcast.35), calls=%async_computation.4 | async-start | bytes 4194304 | tf_op jit(solution)/shard_map/all_to_all | solution.py:376
  93.4 2.1 %copy-start.10 = (bf16[4,128,2048]{2,1,0:T(8,128)(2,1)S(1)}, bf16[4,128,2048]{2,1,0:T(8,128)(2,1)}, u32[]{:S(2)}) copy-start(bf16[4,128,2048]{2,1,0:T(8,128)(2,1)} %copy-done.9) | copy-start | bytes 6291460
  93.5 2.2 %copy-start.12 = (bf16[4,64,2048]{2,1,0:T(8,128)(2,1)S(1)}, bf16[4,64,2048]{2,1,0:T(8,128)(2,1)}, u32[]{:S(2)}) copy-start(bf16[4,64,2048]{2,1,0:T(8,128)(2,1)} %copy-done.11) | copy-start | bytes 3145732
  95.1 16.6 %collective-permute-start.3 = (bf16[136,2048]{1,0:T(8,128)(2,1)}, bf16[136,2048]{1,0:T(8,128)(2,1)S(1)}, u32[]{:S(2)}, u32[]{:S(2)}) collective-permute-start(bf16[136,2048]{1,0:T(8,128)(2,1)} %copy-done.13), channel_id=1, source_target_pairs={{0,1},{1,2},{2,3},{3,4},{4,5},{5,6},{6,7},{7,0},{8,9},{9,10},{10,1... | collective-permute-start | bytes 1671176 | tf_op jit(solution)/shard_map/ppermute | solution.py:26
  95.5 16.2 %copy-start.3 = (bf16[2048,64]{1,0:T(8,128)(2,1)}, bf16[2048,64]{1,0:T(8,128)(2,1)S(1)}, u32[]{:S(2)}) copy-start(bf16[2048,64]{1,0:T(8,128)(2,1)S(1)} %maximum_bitcast_fusion.refs_4_.refs_1_) | copy-start | bytes 786436
  95.6 2.0 %copy-start.17 = (bf16[1,1,768,2048]{3,2,1,0:T(8,128)(2,1)S(1)}, bf16[1,1,768,2048]{3,2,1,0:T(8,128)(2,1)}, u32[]{:S(2)}) copy-start(bf16[1,1,768,2048]{3,2,1,0:T(8,128)(2,1)} %param.20) | copy-start | bytes 9437188
  112.8 1.0 copy-start.6
  115.9 14.2 %all-to-all-start.3 = ((bf16[4,64,2048]{2,1,0:T(8,128)(2,1)}), bf16[4,64,2048]{2,1,0:T(8,128)(2,1)}, u32[]{:S(2)}, u32[]{:S(2)}) async-start(bf16[4,64,2048]{2,1,0:T(8,128)(2,1)} %bitcast.36), calls=%async_computation.3 | async-start | bytes 2097152 | tf_op jit(solution)/shard_map/all_to_all | solution.py:376
  121.1 1.0 copy-start.4
  122.2 0.9 copy-start.16
  130.1 1.0 copy-start.5
  133.7 7.2 %collective-permute-start.7 = (f32[32,768]{1,0:T(8,128)S(1)}, f32[32,768]{1,0:T(8,128)S(1)}, u32[]{:S(2)}, u32[]{:S(2)}) collective-permute-start(f32[32,768]{1,0:T(8,128)S(1)} %left_share.3), channel_id=1, source_target_pairs={{0,32},{32,0},{64,96},{96,64},{128,160},{160,128},{192,224},{224,1... | collective-permute-start | bytes 294920 | tf_op jit(solution)/shard_map/ppermute | solution.py:361
  140.9 14.8 %collective-permute-start.8 = (f32[32,768]{1,0:T(8,128)S(1)}, f32[32,768]{1,0:T(8,128)S(1)}, u32[]{:S(2)}, u32[]{:S(2)}) collective-permute-start(f32[32,768]{1,0:T(8,128)S(1)} %add.65.a_ref), channel_id=1, source_target_pairs={{0,64},{32,96},{64,0},{96,32},{128,192},{160,224},{192,128},{224,1... | collective-permute-start | bytes 294920 | tf_op jit(solution)/shard_map/ppermute | solution.py:361
  142.4 13.4 %collective-permute-start.9 = (f32[32,768]{1,0:T(8,128)S(1)}, f32[32,768]{1,0:T(8,128)S(1)}, u32[]{:S(2)}, u32[]{:S(2)}) collective-permute-start(f32[32,768]{1,0:T(8,128)S(1)} %add.65.a_ref), channel_id=1, source_target_pairs={{0,128},{32,160},{64,192},{96,224},{128,0},{160,32},{192,64},{224,... | collective-permute-start | bytes 294920 | tf_op jit(solution)/shard_map/ppermute | solution.py:361
  145.1 10.7 %collective-permute-start.10 = (f32[32,768]{1,0:T(8,128)S(1)}, f32[32,768]{1,0:T(8,128)S(1)}, u32[]{:S(2)}, u32[]{:S(2)}) collective-permute-start(f32[32,768]{1,0:T(8,128)S(1)} %add.65.a_ref), channel_id=1, source_target_pairs={{0,192},{32,224},{64,128},{96,160},{128,64},{160,96},{192,0},{224,... | collective-permute-start | bytes 294920 | tf_op jit(solution)/shard_map/ppermute | solution.py:361
  145.1 2.8 %copy-start.2 = (f32[768,2048]{1,0:T(8,128)S(1)}, f32[768,2048]{1,0:T(8,128)}, u32[]{:S(2)}) copy-start(f32[768,2048]{1,0:T(8,128)} %get-tuple-element.13.refs_2_) | copy-start | bytes 18874372
  159.9 2.2 %collective-permute-start.11 = (f32[32,2048]{1,0:T(8,128)S(1)}, f32[32,2048]{1,0:T(8,128)S(1)}, u32[]{:S(2)}, u32[]{:S(2)}) collective-permute-start(f32[32,2048]{1,0:T(8,128)S(1)} %get-tuple-element.17), channel_id=1, source_target_pairs={{0,32},{32,0},{64,96},{96,64},{128,160},{160,128},{192,224},{224,1... | collective-permute-start | bytes 786440 | tf_op jit(solution)/shard_map/ppermute | solution.py:361
  162.2 4.8 %collective-permute-start.12 = (bf16[32,2048]{1,0:T(8,128)(2,1)S(1)}, bf16[32,2048]{1,0:T(8,128)(2,1)S(1)}, u32[]{:S(2)}, u32[]{:S(2)}) collective-permute-start(bf16[32,2048]{1,0:T(8,128)(2,1)S(1)} %add_convert_fusion.a_ref), channel_id=1, source_target_pairs={{0,64},{32,96},{64,0},{96,32},{128,192},{160,224},{192,128},{224,1... | collective-permute-start | bytes 393224 | tf_op jit(solution)/shard_map/ppermute | solution.py:361
  162.4 10.0 %collective-permute-start.13 = (bf16[32,2048]{1,0:T(8,128)(2,1)S(1)}, bf16[32,2048]{1,0:T(8,128)(2,1)S(1)}, u32[]{:S(2)}, u32[]{:S(2)}) collective-permute-start(bf16[32,2048]{1,0:T(8,128)(2,1)S(1)} %add_convert_fusion.a_ref), channel_id=1, source_target_pairs={{0,128},{32,160},{64,192},{96,224},{128,0},{160,32},{192,64},{224,... | collective-permute-start | bytes 393224 | tf_op jit(solution)/shard_map/ppermute | solution.py:361
  166.3 8.6 %collective-permute-start.14 = (bf16[32,2048]{1,0:T(8,128)(2,1)S(1)}, bf16[32,2048]{1,0:T(8,128)(2,1)S(1)}, u32[]{:S(2)}, u32[]{:S(2)}) collective-permute-start(bf16[32,2048]{1,0:T(8,128)(2,1)S(1)} %add_convert_fusion.a_ref), channel_id=1, source_target_pairs={{0,192},{32,224},{64,128},{96,160},{128,64},{160,96},{192,0},{224,... | collective-permute-start | bytes 393224 | tf_op jit(solution)/shard_map/ppermute | solution.py:361

commit v3 on v2

--- a/solution.py
+++ b/solution.py
@@ -223,23 +223,28 @@
     )(order, hidden, *parts, q_turned, p_rest)
 
 
-def tail_kernel(count, sources, tile, order, hidden_hbm, *refs):
+def turn_kernel(sources, order, hidden_ref, after_ref, out_ref):
+    turn(order, hidden_ref, out_ref, sources)
+
+
+def turn_last(order, hidden, after):
+    vmem, far = pl.BlockSpec(memory_space=pltpu.VMEM), pl.BlockSpec(memory_space=pl.ANY)
+    feats = hidden.shape[1]
+    sources = order.shape[0]
+    return pl.pallas_call(
+        functools.partial(turn_kernel, sources),
+        in_specs=[pl.BlockSpec(memory_space=pltpu.SMEM), vmem, far],
+        out_specs=vmem,
+        out_shape=jax.ShapeDtypeStruct((feats, sources * CAP), BF16),
+        cost_estimate=pl.CostEstimate(flops=0, bytes_accessed=4 << 20, transcendentals=0),
+        compiler_params=pltpu.CompilerParams(vmem_limit_bytes=16 << 20),
+        name="turn_last",
+    )(order, hidden, after)
+
+
+def tail_kernel(count, tile, turned, *refs):
     parts = refs[:count]
-    acc_ref, high_ref, low_ref, held, turned, sem = refs[count:]
-    copies = [
-        pltpu.make_async_copy(
-            hidden_hbm.at[pl.ds(pl.multiple_of(order[j] * CAP, CAP), CAP)],
-            held.at[pl.ds(j * CAP, CAP)],
-            sem.at[j],
-        )
-        for j in range(sources)
-    ]
-    for copy in copies:
-        copy.start()
-    for copy in copies:
-        copy.wait()
-    for j in range(0, sources * CAP, 2 * CAP):
-        turned[:, j : j + 2 * CAP] = held[j : j + 2 * CAP, :].T
+    acc_ref, high_ref, low_ref = refs[count:]
 
     @pl.loop(0, acc_ref.shape[1] // tile)
     def _(i):
@@ -249,30 +254,23 @@
         high_ref[:, cols], low_ref[:, cols] = split(acc)
 
 
-def tail(order, hidden, parts, acc, tile=256):
+def tail(turned, parts, acc, tile=256):
     rows, width = acc.shape
-    feats = hidden.shape[1]
-    sources = order.shape[0]
+    depth = turned.shape[1]
     vmem = pl.BlockSpec(memory_space=pltpu.VMEM)
     return pl.pallas_call(
-        functools.partial(tail_kernel, len(parts), sources, tile),
-        in_specs=[pl.BlockSpec(memory_space=pltpu.SMEM), pl.BlockSpec(memory_space=pl.ANY)]
-        + [vmem] * (len(parts) + 1),
+        functools.partial(tail_kernel, len(parts), tile),
+        in_specs=[vmem] * (len(parts) + 2),
         out_specs=[vmem, vmem],
-        scratch_shapes=[
-            pltpu.VMEM((sources * CAP, feats), BF16),
-            pltpu.VMEM((feats, sources * CAP), BF16),
-            pltpu.SemaphoreType.DMA((sources,)),
-        ],
         out_shape=[jax.ShapeDtypeStruct((rows, width), BF16)] * 2,
         cost_estimate=pl.CostEstimate(
-            flops=2 * feats * sources * CAP * width,
-            bytes_accessed=rows * width * 8 + sources * CAP * (feats + width) * 2,
+            flops=2 * rows * depth * width,
+            bytes_accessed=rows * width * 8 + depth * (rows + width) * 2,
             transcendentals=0,
         ),
-        compiler_params=pltpu.CompilerParams(vmem_limit_bytes=32 << 20),
+        compiler_params=pltpu.CompilerParams(vmem_limit_bytes=24 << 20),
         name="tail",
-    )(order, hidden, *parts, acc)
+    )(turned, *parts, acc)
 
 
 def factors_kernel(a_ref, b_ref, c_ref, d_ref, high_ref, low_ref, p_ref, q_ref, turned_ref):
@@ -389,9 +387,12 @@
     b[5] = move(b[6], 0, -1)
     b[4] = move(b[3], 0, 1)
     spread(GROUPS[0], select([own], ids))
-    for group in GROUPS[1:4]:
-        spread(group, select([b[k] for k in group], ids))
     held = hidden[0, 0]
+    dx = jnp.array([i for group in GROUPS[3:] for i in range(NX) for k in group], jnp.int32)
+    dz = jnp.array([k for group in GROUPS[3:] for i in range(NX) for k in group], jnp.int32)
+    turned = turn_last(dx * NZ + (z - dz) % NZ, held, own)
+    for group, after in zip(GROUPS[1:4], ((), (), (turned,))):
+        spread(group, select([b[k] for k in group], ids, after))
     q_turned = jnp.concatenate(split(q_init[0]), axis=0).T
     acc, p_rest = product(jnp.concatenate(order[:3]), held, parts[:3], error[0, 0], q_turned)
     spread(GROUPS[4], select([b[k] for k in GROUPS[4]], ids, (p_rest,)))
@@ -399,7 +400,7 @@
     p_local = left_share(order[4], held, parts[4:], q_turned, p_rest)
     p_chip = p_local + partner(p_local, 1)
     p_parts = [p_chip] + [partner(p_chip, k) for k in (2, 4, 6)]
-    high, low = tail(jnp.concatenate(order[3:]), held, parts[3:], acc)
+    high, low = tail(turned, parts[3:], acc)
     p_hat, q_local, p_turned = factors(p_parts, high, low)
     q_chip = (q_local + partner(q_local, 1)).astype(BF16)
     new_error, q_mean = finish(p_turned, [q_chip] + [partner(q_chip, k) for k in (2, 4, 6)], high, low)

time: 179 us -> 178 us (level)
  local copies, waits for them, and re-layouts: 16 us -> 20.7 us
  waiting for transfers between devices: 61.1 us -> 57.4 us
  Pallas kernels: 48.7 us -> 46.3 us
    unnamed x47 -> x57, local copies, waits for them, and re-layouts: 15.2 us -> 19.9 us
    all_to_all x5, waiting for transfers between devices: 19.7 us -> 17.7 us  [spread(): lax.all_to_all(sent, 'exp', split_axis=0, concat_axis=0, tiled=True, axis...]
    ppermute x7, waiting for transfers between devices: 30.8 us -> 29 us  [move(): return lax.ppermute(block, 'exp', pairs)]
    pallas_call x1 -> x2, Pallas kernels: 7.89 us -> 6.75 us  [the longest x1 5.85 us: tail(): pl.pallas_call(functools.partial(tail_kernel, len(parts), tile), in_specs...]
  transfers between devices with their start and end apart: 20 -> 20, of which waited for: 12 -> 12; matrix products, arithmetic and copies ran while one was open for 2% -> 2% of each run, Pallas kernels for 20% -> 18%
where the time goes in v3:
time: 178 us; the launch traced here: 177 us
  waiting for transfers between devices  57.4 us (32%)
  starting transfers between devices  49.3 us (28%)
  Pallas kernels  46.3 us (26%)
  local copies, waits for them, and re-layouts  20.7 us (12%)
  other arithmetic  1.96 us (1%)
    ppermute x7, waiting for transfers between devices, move(): return lax.ppermute(block, 'exp', pairs)  29 us
    all_to_all x5, starting transfers between devices, spread(): lax.all_to_all(sent, 'exp', split_axis=0, concat_axis=0, tiled=True, axis...  22.3 us
    unnamed x57, local copies, waits for them, and re-layouts  19.9 us
    all_to_all x5, waiting for transfers between devices, spread(): lax.all_to_all(sent, 'exp', split_axis=0, concat_axis=0, tiled=True, axis...  17.7 us
    ppermute x8, starting transfers between devices, partner(): return lax.ppermute(value, 'rep', [(i, i ^ k) for i in range(8)])  15.6 us
    pallas_call x1, Pallas kernels, product(): pl.pallas_call(functools.partial(product_kernel, len(parts), sources), gr...  14 us
    ppermute x7, starting transfers between devices, move(): return lax.ppermute(block, 'exp', pairs)  11.3 us
    ppermute x8, waiting for transfers between devices, partner(): return lax.ppermute(value, 'rep', [(i, i ^ k) for i in range(8)])  10.7 us
  transfers between devices with their start and end apart: 20, of which 12 were waited for; matrix products, arithmetic and copies ran while one was open for 2% of the time, Pallas kernels for 18%

profile of v3, /device:TPU:1, one launch (start us, length us, event | category | flops | bytes accessed | tf_op | source)
XLA Modules:
  0.0 176.7 jit_solution(5989073076549024375)
XLA Ops:
  0.7 1.9 %pack.1.refs_0_.after_ref = bf16[136,2048]{1,0:T(8,128)(2,1)} custom-call(bf16[128,2048]{1,0:T(8,128)(2,1)} %bitcast.42, s32[8,128]{1,0:T(8,128)} %bitcast.43, f32[8,128]{1,0:T(8,128)} %bitcast.44), custom_call_target="tpu_custom_call" | custom-call | bytes 1048576 | tf_op jit(solution)/shard_map/pack/pallas_call | solution.py:103
  2.6 1.1 copy-done.6
  3.6 2.1 %select.19 = bf16[256,2048]{1,0:T(8,128)(2,1)} custom-call(s32[4]{0:T(128)S(1)} %fusion.9.ids_ref, bf16[136,2048]{1,0:T(8,128)(2,1)S(1)} %copy-done.6), custom_call_target="tpu_custom_call" | custom-call | flops 134217728 | bytes 1605632 | tf_op jit(solution)/shard_map/select/pallas_call | solution.py:73
  5.7 4.8 %all-to-all-start = ((bf16[4,64,2048]{2,1,0:T(8,128)(2,1)}), bf16[4,64,2048]{2,1,0:T(8,128)(2,1)S(1)}, u32[]{:S(2)}, u32[]{:S(2)}) async-start(bf16[4,64,2048]{2,1,0:T(8,128)(2,1)} %bitcast.6), calls=%async_computation | async-start | bytes 2097152 | tf_op jit(solution)/shard_map/all_to_all | solution.py:374
  10.6 1.6 collective-permute-start
  12.2 4.0 %collective-permute-start.4 = (bf16[136,2048]{1,0:T(8,128)(2,1)S(1)}, bf16[136,2048]{1,0:T(8,128)(2,1)S(1)}, u32[]{:S(2)}, u32[]{:S(2)}) collective-permute-start(bf16[136,2048]{1,0:T(8,128)(2,1)S(1)} %copy-done.7), channel_id=1, source_target_pairs={{0,7},{1,0},{2,1},{3,2},{4,3},{5,4},{6,5},{7,6},{8,15},{9,8},{10,9... | collective-permute-start | bytes 1671176 | tf_op jit(solution)/shard_map/ppermute | solution.py:26
  16.3 11.9 %collective-permute-done.refs_0_ = bf16[136,2048]{1,0:T(8,128)(2,1)S(1)} collective-permute-done((bf16[136,2048]{1,0:T(8,128)(2,1)S(1)}, bf16[136,2048]{1,0:T(8,128)(2,1)S(1)}, u32[]{:S(2)}, u32[]{:S(2)}) %collective-permute-start) | collective-permute-done | bytes 557088 | tf_op jit(solution)/shard_map/ppermute | solution.py:26
  28.2 2.8 %select.20 = bf16[512,2048]{1,0:T(8,128)(2,1)} custom-call(s32[4]{0:T(128)S(1)} %fusion.9.ids_ref, bf16[136,2048]{1,0:T(8,128)(2,1)S(1)} %collective-permute-done.refs_0_, bf16[136,2048]{1,0:T(8,128)(2,1)S(1)} %collective-permute-done.4.refs_1_), custom_call_target="tpu_custom_call" | custom-call | flops 268435456 | bytes 3211264 | tf_op jit(solution)/shard_map/select/pallas_call | solution.py:73
  32.0 3.9 %all-to-all-start.1 = ((bf16[4,128,2048]{2,1,0:T(8,128)(2,1)}), bf16[4,128,2048]{2,1,0:T(8,128)(2,1)S(1)}, u32[]{:S(2)}, u32[]{:S(2)}) async-start(bf16[4,128,2048]{2,1,0:T(8,128)(2,1)} %bitcast.8), calls=%async_computation.1 | async-start | bytes 4194304 | tf_op jit(solution)/shard_map/all_to_all | solution.py:374
  35.9 2.7 %collective-permute-start.5 = (bf16[136,2048]{1,0:T(8,128)(2,1)S(1)}, bf16[136,2048]{1,0:T(8,128)(2,1)S(1)}, u32[]{:S(2)}, u32[]{:S(2)}) collective-permute-start(bf16[136,2048]{1,0:T(8,128)(2,1)S(1)} %collective-permute-done.4.refs_1_), channel_id=1, source_target_pairs={{0,7},{1,0},{2,1},{3,2},{4,3},{5,4},{6,5},{7,6},{8,15},{9,8},{10,9... | collective-permute-start | bytes 1671176 | tf_op jit(solution)/shard_map/ppermute | solution.py:26
  38.6 10.5 %collective-permute-done.1.refs_0_ = bf16[136,2048]{1,0:T(8,128)(2,1)S(1)} collective-permute-done((bf16[136,2048]{1,0:T(8,128)(2,1)S(1)}, bf16[136,2048]{1,0:T(8,128)(2,1)S(1)}, u32[]{:S(2)}, u32[]{:S(2)}) %collective-permute-start.1) | collective-permute-done | bytes 557088 | tf_op jit(solution)/shard_map/ppermute | solution.py:26
  49.0 1.5 select.21
  50.6 1.3 copy-done.3
  53.5 6.5 %all-to-all-done.1 = bf16[4,128,2048]{2,1,0:T(8,128)(2,1)S(1)} async-done(((bf16[4,128,2048]{2,1,0:T(8,128)(2,1)}), bf16[4,128,2048]{2,1,0:T(8,128)(2,1)S(1)}, u32[]{:S(2)}, u32[]{:S(2)}) %all-to-all-start.1) | async-done | bytes 2097184 | tf_op jit(solution)/shard_map/all_to_all | solution.py:374
  60.1 1.3 copy-done.13
  61.4 4.7 %all-to-all-start.2 = ((bf16[4,128,2048]{2,1,0:T(8,128)(2,1)}), bf16[4,128,2048]{2,1,0:T(8,128)(2,1)}, u32[]{:S(2)}, u32[]{:S(2)}) async-start(bf16[4,128,2048]{2,1,0:T(8,128)(2,1)} %bitcast.35), calls=%async_computation.2 | async-start | bytes 4194304 | tf_op jit(solution)/shard_map/all_to_all | solution.py:374
  66.2 2.7 %collective-permute-start.6 = (bf16[136,2048]{1,0:T(8,128)(2,1)}, bf16[136,2048]{1,0:T(8,128)(2,1)}, u32[]{:S(2)}, u32[]{:S(2)}) collective-permute-start(bf16[136,2048]{1,0:T(8,128)(2,1)} %copy-done.18), channel_id=1, source_target_pairs={{0,7},{1,0},{2,1},{3,2},{4,3},{5,4},{6,5},{7,6},{8,15},{9,8},{10,9... | collective-permute-start | bytes 1671176 | tf_op jit(solution)/shard_map/ppermute | solution.py:26
  68.9 1.3 copy.21
  70.2 1.0 copy-done.8
  72.2 6.6 %collective-permute-done.2.refs_0_ = bf16[136,2048]{1,0:T(8,128)(2,1)} collective-permute-done((bf16[136,2048]{1,0:T(8,128)(2,1)}, bf16[136,2048]{1,0:T(8,128)(2,1)}, u32[]{:S(2)}, u32[]{:S(2)}) %collective-permute-start.2) | collective-permute-done | bytes 557088 | tf_op jit(solution)/shard_map/ppermute | solution.py:26
  78.8 2.2 %select.23 = bf16[512,2048]{1,0:T(8,128)(2,1)S(1)} custom-call(s32[4]{0:T(128)S(1)} %fusion.9.ids_ref, bf16[136,2048]{1,0:T(8,128)(2,1)} %collective-permute-done.2.refs_0_, bf16[136,2048]{1,0:T(8,128)(2,1)} %collective-permute-done.6.refs_1_, bf16[768,768]{1,0:T(8,128)(2,1)S(1)} %turn_last.1.refs_2_.turned), custom_call_target="tpu_custom_call" | custom-call | flops 268435456 | bytes 3211264 | tf_op jit(solution)/shard_map/select/pallas_call | solution.py:73
  81.0 1.0 copy-done.1
  82.0 1.4 copy-done.4
  83.4 6.1 %all-to-all-done.2 = bf16[4,128,2048]{2,1,0:T(8,128)(2,1)} async-done(((bf16[4,128,2048]{2,1,0:T(8,128)(2,1)}), bf16[4,128,2048]{2,1,0:T(8,128)(2,1)}, u32[]{:S(2)}, u32[]{:S(2)}) %all-to-all-start.2) | async-done | bytes 2097184 | tf_op jit(solution)/shard_map/all_to_all | solution.py:374
  89.5 4.6 %all-to-all-start.4 = ((bf16[4,128,2048]{2,1,0:T(8,128)(2,1)}), bf16[4,128,2048]{2,1,0:T(8,128)(2,1)}, u32[]{:S(2)}, u32[]{:S(2)}) async-start(bf16[4,128,2048]{2,1,0:T(8,128)(2,1)} %bitcast.36), calls=%async_computation.4 | async-start | bytes 4194304 | tf_op jit(solution)/shard_map/all_to_all | solution.py:374
  94.2 1.5 fusion
  96.4 2.1 %copy-done.20 = bf16[1,1,768,2048]{3,2,1,0:T(8,128)(2,1)S(1)} copy-done((bf16[1,1,768,2048]{3,2,1,0:T(8,128)(2,1)S(1)}, bf16[1,1,768,2048]{3,2,1,0:T(8,128)(2,1)}, u32[]{:S(2)}) %copy-start.20) | copy-done | bytes 3145752
  98.4 14.0 %product.1 = (f32[768,2048]{1,0:T(8,128)}, f32[768,32]{1,0:T(8,128)S(1)}) custom-call(s32[20]{0:T(128)S(1)} %pad_add_fusion.order, bf16[2048,768]{1,0:T(8,128)(2,1)S(1)} %bitcast.32, bf16[256,2048]{1,0:T(8,128)(2,1)S(1)} %bitcast.39, bf16[512,2048]{1,0:T(8,128)(2,1)S(1)} %bitcast.38, bf16[512,2048]{1,0:T(8,128)(2,1)} %bitcast.11.refs_2_, ...), custom_call_target="tpu_custom_call" | custom-call | flops 4026531840 | bytes 19791872 | tf_op jit(solution)/shard_map/product/pallas_call | solution.py:154
  112.4 1.1 select.22
  114.5 1.9 %all-to-all-done.4 = bf16[4,128,2048]{2,1,0:T(8,128)(2,1)} async-done(((bf16[4,128,2048]{2,1,0:T(8,128)(2,1)}), bf16[4,128,2048]{2,1,0:T(8,128)(2,1)}, u32[]{:S(2)}, u32[]{:S(2)}) %all-to-all-start.4) | async-done | bytes 2097184 | tf_op jit(solution)/shard_map/all_to_all | solution.py:374
  116.5 4.2 %all-to-all-start.3 = ((bf16[4,64,2048]{2,1,0:T(8,128)(2,1)}), bf16[4,64,2048]{2,1,0:T(8,128)(2,1)}, u32[]{:S(2)}, u32[]{:S(2)}) async-start(bf16[4,64,2048]{2,1,0:T(8,128)(2,1)} %bitcast.37), calls=%async_computation.3 | async-start | bytes 2097152 | tf_op jit(solution)/shard_map/all_to_all | solution.py:374
  121.5 1.0 copy-done.10
  123.5 4.0 %left_share.2.refs_2_ = f32[32,768]{1,0:T(8,128)S(1)} custom-call(s32[8]{0:T(128)S(1)} %get-tuple-element.23.order, bf16[2048,768]{1,0:T(8,128)(2,1)S(1)} %bitcast.33, bf16[512,2048]{1,0:T(8,128)(2,1)} %bitcast.18.refs_0_, bf16[2048,64]{1,0:T(8,128)(2,1)S(1)} %copy-done.10, f32[32,768]{1,0:T(8,128)S(1)} %bitcast.40), custom_call_target="tpu_custom_call" | custom-call | tf_op jit(solution)/shard_map/left_share/pallas_call | solution.py:211
  127.5 3.1 %all-to-all-done.3 = bf16[4,64,2048]{2,1,0:T(8,128)(2,1)} async-done(((bf16[4,64,2048]{2,1,0:T(8,128)(2,1)}), bf16[4,64,2048]{2,1,0:T(8,128)(2,1)}, u32[]{:S(2)}, u32[]{:S(2)}) %all-to-all-start.3) | async-done | bytes 1048608 | tf_op jit(solution)/shard_map/all_to_all | solution.py:374
  130.6 1.0 copy-done.11
  131.7 2.7 %left_share.3 = f32[32,768]{1,0:T(8,128)S(1)} custom-call(s32[4]{0:T(128)S(1)} %fusion.11.order, bf16[2048,768]{1,0:T(8,128)(2,1)S(1)} %bitcast.34, bf16[256,2048]{1,0:T(8,128)(2,1)} %bitcast.16.refs_0_.refs_1_, bf16[2048,64]{1,0:T(8,128)(2,1)S(1)} %copy-done.11, f32[32,768]{1,0:T(8,128)S(1)} %left_share.2.refs_2_), custom_call_target="tpu_custom_call" | custom-call | tf_op jit(solution)/shard_map/left_share/pallas_call | solution.py:211
  134.4 6.3 %collective-permute-start.7 = (f32[32,768]{1,0:T(8,128)S(1)}, f32[32,768]{1,0:T(8,128)S(1)}, u32[]{:S(2)}, u32[]{:S(2)}) collective-permute-start(f32[32,768]{1,0:T(8,128)S(1)} %left_share.3), channel_id=1, source_target_pairs={{0,32},{32,0},{64,96},{96,64},{128,160},{160,128},{192,224},{224,1... | collective-permute-start | bytes 294920 | tf_op jit(solution)/shard_map/ppermute | solution.py:359
  141.6 1.5 collective-permute-start.8
  143.1 2.7 %collective-permute-start.9 = (f32[32,768]{1,0:T(8,128)S(1)}, f32[32,768]{1,0:T(8,128)S(1)}, u32[]{:S(2)}, u32[]{:S(2)}) collective-permute-start(f32[32,768]{1,0:T(8,128)S(1)} %add.76.a_ref), channel_id=1, source_target_pairs={{0,128},{32,160},{64,192},{96,224},{128,0},{160,32},{192,64},{224,... | collective-permute-start | bytes 294920 | tf_op jit(solution)/shard_map/ppermute | solution.py:359
  145.8 2.8 %copy-done.5 = f32[768,2048]{1,0:T(8,128)S(1)} copy-done((f32[768,2048]{1,0:T(8,128)S(1)}, f32[768,2048]{1,0:T(8,128)}, u32[]{:S(2)}) %copy-start.5) | copy-done | bytes 6291480
  148.6 5.8 %tail.1 = (bf16[768,2048]{1,0:T(8,128)(2,1)S(1)}, bf16[768,2048]{1,0:T(8,128)(2,1)S(1)}) custom-call(bf16[768,768]{1,0:T(8,128)(2,1)S(1)} %copy-done.2, bf16[512,2048]{1,0:T(8,128)(2,1)} %bitcast.18.refs_0_, bf16[256,2048]{1,0:T(8,128)(2,1)} %bitcast.16.refs_0_.refs_1_, f32[768,2048]{1,0:T(8,128)S(1)} %copy-done.5), custom_call_target="tpu_custom_call" | custom-call | flops 2415919104 | bytes 16908288 | tf_op jit(solution)/shard_map/tail/pallas_call | solution.py:261
  154.5 4.2 %factors.1 = (f32[32,768]{1,0:T(8,128)}, f32[32,2048]{1,0:T(8,128)S(1)}, bf16[768,96]{1,0:T(8,128)(2,1)S(1)}) custom-call(f32[32,768]{1,0:T(8,128)S(1)} %add.76.a_ref, f32[32,768]{1,0:T(8,128)S(1)} %collective-permute-done.8.b_ref, f32[32,768]{1,0:T(8,128)S(1)} %collective-permute-done.9.c_ref, f32[32,768]{1,0:T(8,128)S(1)} %collective-permute-done.10.d_ref, ...), custom_call_target="tpu_custom_call" | custom-call | tf_op jit(solution)/shard_map/factors/pallas_call | solution.py:301
  158.6 1.0 collective-permute-start.11
  159.7 1.2 collective-permute-done.11
  161.1 3.9 %collective-permute-start.13 = (bf16[32,2048]{1,0:T(8,128)(2,1)S(1)}, bf16[32,2048]{1,0:T(8,128)(2,1)S(1)}, u32[]{:S(2)}, u32[]{:S(2)}) collective-permute-start(bf16[32,2048]{1,0:T(8,128)(2,1)S(1)} %add_convert_fusion.a_ref), channel_id=1, source_target_pairs={{0,128},{32,160},{64,192},{96,224},{128,0},{160,32},{192,64},{224,... | collective-permute-start | bytes 393224 | tf_op jit(solution)/shard_map/ppermute | solution.py:359
  165.7 5.4 %collective-permute-done.13.c_ref = bf16[32,2048]{1,0:T(8,128)(2,1)S(1)} collective-permute-done((bf16[32,2048]{1,0:T(8,128)(2,1)S(1)}, bf16[32,2048]{1,0:T(8,128)(2,1)S(1)}, u32[]{:S(2)}, u32[]{:S(2)}) %collective-permute-start.13) | collective-permute-done | bytes 131104 | tf_op jit(solution)/shard_map/ppermute | solution.py:359
  171.1 2.5 %collective-permute-done.14.d_ref = bf16[32,2048]{1,0:T(8,128)(2,1)S(1)} collective-permute-done((bf16[32,2048]{1,0:T(8,128)(2,1)S(1)}, bf16[32,2048]{1,0:T(8,128)(2,1)S(1)}, u32[]{:S(2)}, u32[]{:S(2)}) %collective-permute-start.14) | collective-permute-done | bytes 131104 | tf_op jit(solution)/shard_map/ppermute | solution.py:359
  173.6 2.9 %finish.1 = (bf16[768,2048]{1,0:T(8,128)(2,1)}, f32[32,2048]{1,0:T(8,128)}) custom-call(bf16[768,96]{1,0:T(8,128)(2,1)S(1)} %get-tuple-element.16.p_ref, bf16[32,2048]{1,0:T(8,128)(2,1)S(1)} %add_convert_fusion.a_ref, bf16[32,2048]{1,0:T(8,128)(2,1)S(1)} %collective-permute-done.12.b_ref, bf16[32,2048]{1,0:T(8,128)(2,1)S(1)} %collective-permute-done.13.c_ref, ...), custom_call_target="tpu_custom_call" | custom-call | tf_op jit(solution)/shard_map/finish/pallas_call | solution.py:341
  (73 shorter events, 8.9 us)
Async XLA Ops:
  2.6 1.1 copy-start.6
  3.6 7.0 %copy-start.7 = (bf16[136,2048]{1,0:T(8,128)(2,1)S(1)}, bf16[136,2048]{1,0:T(8,128)(2,1)}, u32[]{:S(2)}) copy-start(bf16[136,2048]{1,0:T(8,128)(2,1)} %pack.1.refs_0_.after_ref) | copy-start | bytes 1671172
  5.7 25.3 %all-to-all-start = ((bf16[4,64,2048]{2,1,0:T(8,128)(2,1)}), bf16[4,64,2048]{2,1,0:T(8,128)(2,1)S(1)}, u32[]{:S(2)}, u32[]{:S(2)}) async-start(bf16[4,64,2048]{2,1,0:T(8,128)(2,1)} %bitcast.6), calls=%async_computation | async-start | bytes 2097152 | tf_op jit(solution)/shard_map/all_to_all | solution.py:374
  10.6 17.6 %collective-permute-start = (bf16[136,2048]{1,0:T(8,128)(2,1)S(1)}, bf16[136,2048]{1,0:T(8,128)(2,1)S(1)}, u32[]{:S(2)}, u32[]{:S(2)}) collective-permute-start(bf16[136,2048]{1,0:T(8,128)(2,1)S(1)} %copy-done.7), channel_id=1, source_target_pairs={{0,1},{1,2},{2,3},{3,4},{4,5},{5,6},{6,7},{7,0},{8,9},{9,10},{10,1... | collective-permute-start | bytes 1671176 | tf_op jit(solution)/shard_map/ppermute | solution.py:26
  12.2 15.9 %collective-permute-start.4 = (bf16[136,2048]{1,0:T(8,128)(2,1)S(1)}, bf16[136,2048]{1,0:T(8,128)(2,1)S(1)}, u32[]{:S(2)}, u32[]{:S(2)}) collective-permute-start(bf16[136,2048]{1,0:T(8,128)(2,1)S(1)} %copy-done.7), channel_id=1, source_target_pairs={{0,7},{1,0},{2,1},{3,2},{4,3},{5,4},{6,5},{7,6},{8,15},{9,8},{10,9... | collective-permute-start | bytes 1671176 | tf_op jit(solution)/shard_map/ppermute | solution.py:26
  31.0 1.0 copy-start.15
  32.0 28.1 %all-to-all-start.1 = ((bf16[4,128,2048]{2,1,0:T(8,128)(2,1)}), bf16[4,128,2048]{2,1,0:T(8,128)(2,1)S(1)}, u32[]{:S(2)}, u32[]{:S(2)}) async-start(bf16[4,128,2048]{2,1,0:T(8,128)(2,1)} %bitcast.8), calls=%async_computation.1 | async-start | bytes 4194304 | tf_op jit(solution)/shard_map/all_to_all | solution.py:374
  35.9 13.1 %collective-permute-start.1 = (bf16[136,2048]{1,0:T(8,128)(2,1)S(1)}, bf16[136,2048]{1,0:T(8,128)(2,1)S(1)}, u32[]{:S(2)}, u32[]{:S(2)}) collective-permute-start(bf16[136,2048]{1,0:T(8,128)(2,1)S(1)} %collective-permute-done.refs_0_), channel_id=1, source_target_pairs={{0,1},{1,2},{2,3},{3,4},{4,5},{5,6},{6,7},{7,0},{8,9},{9,10},{10,1... | collective-permute-start | bytes 1671176 | tf_op jit(solution)/shard_map/ppermute | solution.py:26
  35.9 13.1 %collective-permute-start.5 = (bf16[136,2048]{1,0:T(8,128)(2,1)S(1)}, bf16[136,2048]{1,0:T(8,128)(2,1)S(1)}, u32[]{:S(2)}, u32[]{:S(2)}) collective-permute-start(bf16[136,2048]{1,0:T(8,128)(2,1)S(1)} %collective-permute-done.4.refs_1_), channel_id=1, source_target_pairs={{0,7},{1,0},{2,1},{3,2},{4,3},{5,4},{6,5},{7,6},{8,15},{9,8},{10,9... | collective-permute-start | bytes 1671176 | tf_op jit(solution)/shard_map/ppermute | solution.py:26
  50.6 1.3 copy-start.3
  51.9 0.8 copy-start.17
  52.7 0.8 copy-start.18
  60.1 1.3 copy-start.13
  61.4 7.5 %copy-start.21 = (f32[1,32,2048]{2,1,0:T(8,128)S(1)}, f32[1,32,2048]{2,1,0:T(8,128)}, u32[]{:S(2)}) copy-start(f32[1,32,2048]{2,1,0:T(8,128)} %param.23) | copy-start | bytes 786436
  61.4 8.8 %copy-start.22 = (s32[12]{0:T(128)S(1)}, s32[12]{0:T(128)}, u32[]{:S(2)}) copy-start(s32[12]{0:T(128)} %constant.96) | copy-start | bytes 148
  61.4 8.8 %copy-start.23 = (s32[12]{0:T(128)S(1)}, s32[12]{0:T(128)}, u32[]{:S(2)}) copy-start(s32[12]{0:T(128)} %constant.97) | copy-start | bytes 148
  61.4 8.8 %copy-start = (bf16[1,1,2048,768]{3,2,1,0:T(8,128)(2,1)S(1)}, bf16[1,1,2048,768]{3,2,1,0:T(8,128)(2,1)}, u32[]{:S(2)}) copy-start(bf16[1,1,2048,768]{3,2,1,0:T(8,128)(2,1)} %param.21) | copy-start | bytes 9437188
  61.4 28.0 %all-to-all-start.2 = ((bf16[4,128,2048]{2,1,0:T(8,128)(2,1)}), bf16[4,128,2048]{2,1,0:T(8,128)(2,1)}, u32[]{:S(2)}, u32[]{:S(2)}) async-start(bf16[4,128,2048]{2,1,0:T(8,128)(2,1)} %bitcast.35), calls=%async_computation.2 | async-start | bytes 4194304 | tf_op jit(solution)/shard_map/all_to_all | solution.py:374
  66.1 12.6 %collective-permute-start.2 = (bf16[136,2048]{1,0:T(8,128)(2,1)}, bf16[136,2048]{1,0:T(8,128)(2,1)}, u32[]{:S(2)}, u32[]{:S(2)}) collective-permute-start(bf16[136,2048]{1,0:T(8,128)(2,1)} %copy-done.17), channel_id=1, source_target_pairs={{0,1},{1,2},{2,3},{3,4},{4,5},{5,6},{6,7},{7,0},{8,9},{9,10},{10,1... | collective-permute-start | bytes 1671176 | tf_op jit(solution)/shard_map/ppermute | solution.py:26
  66.2 12.5 %collective-permute-start.6 = (bf16[136,2048]{1,0:T(8,128)(2,1)}, bf16[136,2048]{1,0:T(8,128)(2,1)}, u32[]{:S(2)}, u32[]{:S(2)}) collective-permute-start(bf16[136,2048]{1,0:T(8,128)(2,1)} %copy-done.18), channel_id=1, source_target_pairs={{0,7},{1,0},{2,1},{3,2},{4,3},{5,4},{6,5},{7,6},{8,15},{9,8},{10,9... | collective-permute-start | bytes 1671176 | tf_op jit(solution)/shard_map/ppermute | solution.py:26
  70.2 1.1 copy-start.8
  80.9 1.0 copy-start.1
  82.0 1.4 copy-start.4
  89.4 4.6 %copy-start.24 = (s32[8]{0:T(128)S(1)}, s32[8]{0:T(128)}, u32[]{:S(2)}) copy-start(s32[8]{0:T(128)} %constant.92) | copy-start | bytes 100
  89.4 4.7 %copy-start.25 = (s32[8]{0:T(128)S(1)}, s32[8]{0:T(128)}, u32[]{:S(2)}) copy-start(s32[8]{0:T(128)} %constant.95) | copy-start | bytes 100
  89.5 4.7 %copy-start.26 = (s32[8]{0:T(128)S(1)}, s32[8]{0:T(128)}, u32[]{:S(2)}) copy-start(s32[8]{0:T(128)} %constant.94) | copy-start | bytes 100
  89.5 4.7 %copy-start.27 = (s32[8]{0:T(128)S(1)}, s32[8]{0:T(128)}, u32[]{:S(2)}) copy-start(s32[8]{0:T(128)} %constant.93) | copy-start | bytes 100
  89.5 27.0 %all-to-all-start.4 = ((bf16[4,128,2048]{2,1,0:T(8,128)(2,1)}), bf16[4,128,2048]{2,1,0:T(8,128)(2,1)}, u32[]{:S(2)}, u32[]{:S(2)}) async-start(bf16[4,128,2048]{2,1,0:T(8,128)(2,1)} %bitcast.36), calls=%async_computation.4 | async-start | bytes 4194304 | tf_op jit(solution)/shard_map/all_to_all | solution.py:374
  94.1 2.3 %copy-start.14 = (bf16[4,128,2048]{2,1,0:T(8,128)(2,1)S(1)}, bf16[4,128,2048]{2,1,0:T(8,128)(2,1)}, u32[]{:S(2)}) copy-start(bf16[4,128,2048]{2,1,0:T(8,128)(2,1)} %copy-done.13) | copy-start | bytes 6291460
  94.1 2.3 %copy-start.16 = (bf16[4,64,2048]{2,1,0:T(8,128)(2,1)S(1)}, bf16[4,64,2048]{2,1,0:T(8,128)(2,1)}, u32[]{:S(2)}) copy-start(bf16[4,64,2048]{2,1,0:T(8,128)(2,1)} %copy-done.15) | copy-start | bytes 3145732
  95.7 16.7 %collective-permute-start.3 = (bf16[136,2048]{1,0:T(8,128)(2,1)}, bf16[136,2048]{1,0:T(8,128)(2,1)S(1)}, u32[]{:S(2)}, u32[]{:S(2)}) collective-permute-start(bf16[136,2048]{1,0:T(8,128)(2,1)} %collective-permute-done.2.refs_0_), channel_id=1, source_target_pairs={{0,1},{1,2},{2,3},{3,4},{4,5},{5,6},{6,7},{7,0},{8,9},{9,10},{10,1... | collective-permute-start | bytes 1671176 | tf_op jit(solution)/shard_map/ppermute | solution.py:26
  96.3 16.1 %copy-start.9 = (bf16[2048,64]{1,0:T(8,128)(2,1)}, bf16[2048,64]{1,0:T(8,128)(2,1)S(1)}, u32[]{:S(2)}) copy-start(bf16[2048,64]{1,0:T(8,128)(2,1)S(1)} %maximum_bitcast_fusion.refs_4_.refs_1_) | copy-start | bytes 786436
  96.3 2.1 %copy-start.20 = (bf16[1,1,768,2048]{3,2,1,0:T(8,128)(2,1)S(1)}, bf16[1,1,768,2048]{3,2,1,0:T(8,128)(2,1)}, u32[]{:S(2)}) copy-start(bf16[1,1,768,2048]{3,2,1,0:T(8,128)(2,1)} %param.22) | copy-start | bytes 9437188
  113.5 1.0 copy-start.12
  116.5 14.2 %all-to-all-start.3 = ((bf16[4,64,2048]{2,1,0:T(8,128)(2,1)}), bf16[4,64,2048]{2,1,0:T(8,128)(2,1)}, u32[]{:S(2)}, u32[]{:S(2)}) async-start(bf16[4,64,2048]{2,1,0:T(8,128)(2,1)} %bitcast.37), calls=%async_computation.3 | async-start | bytes 2097152 | tf_op jit(solution)/shard_map/all_to_all | solution.py:374
  121.5 1.0 copy-start.10
  122.6 0.9 copy-start.19
  130.6 1.0 copy-start.11
  131.7 14.1 %copy-start.2 = (bf16[768,768]{1,0:T(8,128)(2,1)S(1)}, bf16[768,768]{1,0:T(8,128)(2,1)}, u32[]{:S(2)}) copy-start(bf16[768,768]{1,0:T(8,128)(2,1)} %copy-done.1) | copy-start | bytes 3538948
  134.4 7.2 %collective-permute-start.7 = (f32[32,768]{1,0:T(8,128)S(1)}, f32[32,768]{1,0:T(8,128)S(1)}, u32[]{:S(2)}, u32[]{:S(2)}) collective-permute-start(f32[32,768]{1,0:T(8,128)S(1)} %left_share.3), channel_id=1, source_target_pairs={{0,32},{32,0},{64,96},{96,64},{128,160},{160,128},{192,224},{224,1... | collective-permute-start | bytes 294920 | tf_op jit(solution)/shard_map/ppermute | solution.py:359
  141.6 12.8 %collective-permute-start.8 = (f32[32,768]{1,0:T(8,128)S(1)}, f32[32,768]{1,0:T(8,128)S(1)}, u32[]{:S(2)}, u32[]{:S(2)}) collective-permute-start(f32[32,768]{1,0:T(8,128)S(1)} %add.76.a_ref), channel_id=1, source_target_pairs={{0,64},{32,96},{64,0},{96,32},{128,192},{160,224},{192,128},{224,1... | collective-permute-start | bytes 294920 | tf_op jit(solution)/shard_map/ppermute | solution.py:359
  143.1 11.3 %collective-permute-start.9 = (f32[32,768]{1,0:T(8,128)S(1)}, f32[32,768]{1,0:T(8,128)S(1)}, u32[]{:S(2)}, u32[]{:S(2)}) collective-permute-start(f32[32,768]{1,0:T(8,128)S(1)} %add.76.a_ref), channel_id=1, source_target_pairs={{0,128},{32,160},{64,192},{96,224},{128,0},{160,32},{192,64},{224,... | collective-permute-start | bytes 294920 | tf_op jit(solution)/shard_map/ppermute | solution.py:359
  145.8 8.7 %collective-permute-start.10 = (f32[32,768]{1,0:T(8,128)S(1)}, f32[32,768]{1,0:T(8,128)S(1)}, u32[]{:S(2)}, u32[]{:S(2)}) collective-permute-start(f32[32,768]{1,0:T(8,128)S(1)} %add.76.a_ref), channel_id=1, source_target_pairs={{0,192},{32,224},{64,128},{96,160},{128,64},{160,96},{192,0},{224,... | collective-permute-start | bytes 294920 | tf_op jit(solution)/shard_map/ppermute | solution.py:359
  145.8 2.8 %copy-start.5 = (f32[768,2048]{1,0:T(8,128)S(1)}, f32[768,2048]{1,0:T(8,128)}, u32[]{:S(2)}) copy-start(f32[768,2048]{1,0:T(8,128)} %get-tuple-element.13.refs_2_) | copy-start | bytes 18874372
  158.6 2.2 %collective-permute-start.11 = (f32[32,2048]{1,0:T(8,128)S(1)}, f32[32,2048]{1,0:T(8,128)S(1)}, u32[]{:S(2)}, u32[]{:S(2)}) collective-permute-start(f32[32,2048]{1,0:T(8,128)S(1)} %get-tuple-element.17), channel_id=1, source_target_pairs={{0,32},{32,0},{64,96},{96,64},{128,160},{160,128},{192,224},{224,1... | collective-permute-start | bytes 786440 | tf_op jit(solution)/shard_map/ppermute | solution.py:359
  160.9 4.8 %collective-permute-start.12 = (bf16[32,2048]{1,0:T(8,128)(2,1)S(1)}, bf16[32,2048]{1,0:T(8,128)(2,1)S(1)}, u32[]{:S(2)}, u32[]{:S(2)}) collective-permute-start(bf16[32,2048]{1,0:T(8,128)(2,1)S(1)} %add_convert_fusion.a_ref), channel_id=1, source_target_pairs={{0,64},{32,96},{64,0},{96,32},{128,192},{160,224},{192,128},{224,1... | collective-permute-start | bytes 393224 | tf_op jit(solution)/shard_map/ppermute | solution.py:359
  161.1 9.9 %collective-permute-start.13 = (bf16[32,2048]{1,0:T(8,128)(2,1)S(1)}, bf16[32,2048]{1,0:T(8,128)(2,1)S(1)}, u32[]{:S(2)}, u32[]{:S(2)}) collective-permute-start(bf16[32,2048]{1,0:T(8,128)(2,1)S(1)} %add_convert_fusion.a_ref), channel_id=1, source_target_pairs={{0,128},{32,160},{64,192},{96,224},{128,0},{160,32},{192,64},{224,... | collective-permute-start | bytes 393224 | tf_op jit(solution)/shard_map/ppermute | solution.py:359
  165.0 8.6 %collective-permute-start.14 = (bf16[32,2048]{1,0:T(8,128)(2,1)S(1)}, bf16[32,2048]{1,0:T(8,128)(2,1)S(1)}, u32[]{:S(2)}, u32[]{:S(2)}) collective-permute-start(bf16[32,2048]{1,0:T(8,128)(2,1)S(1)} %add_convert_fusion.a_ref), channel_id=1, source_target_pairs={{0,192},{32,224},{64,128},{96,160},{128,64},{160,96},{192,0},{224,... | collective-permute-start | bytes 393224 | tf_op jit(solution)/shard_map/ppermute | solution.py:359
